TPU v7x, 32 devices: a whole 2x2x4 slice. The times are simulated.
32 devices in a mesh: emit: 8 (over z, x), vx: 2 (over y), vy: 2 (over core).
Axes of the slice: x: 2, y: 2, z: 4, core: 2. Of those that a mesh axis runs over, the one named last changes fastest.
Arguments:
- fwd_state: float32 [3, 8, 512, 512], P(None, 'emit', 'vx', 'vy'), may hold values from -6 to 6
- adj_state: float32 [3, 8, 512, 512], P(None, 'emit', 'vx', 'vy'), may hold values from -6 to 6
- courant: float32 [512, 512], P('vx', 'vy'), may hold values from 0.2 to 0.45
- decay_rate: float32 [512, 512], P('vx', 'vy'), may hold values from 0.2 to 0.9
- strength: float32 [512, 512], P('vx', 'vy'), may hold values from 0.05 to 0.4
- footprint: int32 [8, 2, 2, 16], P('emit', 'vx', 'vy'), may hold values from 0 to 31, all different within a row
- owner_map: int32 [2, 2, 32], P('vx', 'vy'), may hold values from 0 to 31, each once within a row
Outputs:
- gradient: float32 [32, 32, 256], P('emit', 'vx', 'vy')
- pressure: float32 [8, 512, 512], P('emit', 'vx', 'vy')
Inputs may be any that keep to these rules, and one draw needn't show every extreme that they name: `footprint`: in each row the 16 ids are distinct block ids of one tile. `owner_map`: for each tile a permutation of its 32 block ids.
All inputs are finite; a program needn't handle non-finite values.
Results may differ from a plain program's by a relative error of at most 0.0003.
Values sent between devices are 32-bit elements; how exact they have to be, the bound alone decides.
A program may use at most 64 MiB of HBM per device.

v0:
```python
import jax
import jax.numpy as jnp
from jax import lax
from jax.sharding import PartitionSpec as P

BR = 16
BC = 128
BX = 16
BY = 2
STEPS = 4


def with_halo(block, sides, width):
    for axis, dim in sides:
        count = lax.axis_size(axis)
        forward = [(i, i + 1) for i in range(count - 1)]
        backward = [(target, source) for source, target in forward]
        low = lax.ppermute(
            lax.slice_in_dim(block, block.shape[dim] - width, None, axis=dim), axis, forward
        )
        high = lax.ppermute(lax.slice_in_dim(block, 0, width, axis=dim), axis, backward)
        block = jnp.concatenate([low, block, high], axis=dim)
    return block


def halo_laplace(field):
    padded = with_halo(field, (("vx", 0), ("vy", 1)), 1)
    return padded[2:, 1:-1] + padded[:-2, 1:-1] + padded[1:-1, 2:] + padded[1:-1, :-2] - 4.0 * field


def keep_all(field):
    return field


def advance(state, courant, decay_rate, strength, laplace_fn):
    former, current, memory = state
    curve = laplace_fn(current)
    memory = decay_rate * memory + strength * curve
    following = 2.0 * current - former + courant * (curve - memory)
    return (current, following, memory)


def propagate(state, courant, decay_rate, strength, laplace_fn, crop):
    levels = [crop(state[0]), crop(state[1])]
    for number in range(STEPS):
        state = advance(state, courant, decay_rate, strength, laplace_fn)
        levels.append(crop(state[1]))
    return levels


def imaging(forward, adjoint, scale):
    result = None
    for level in range(1, STEPS + 1):
        second = forward[level + 1] - 2.0 * forward[level] + forward[level - 1]
        term = adjoint[STEPS + 2 - level] * second
        result = term if result is None else result + term
    return result * scale


def shards(fwd_state, adj_state, courant, decay_rate, strength, footprint, owner_map):
    groups = lax.axis_size("emit")
    blocks_count = owner_map.shape[-1]
    forward_in = (fwd_state[0, 0], fwd_state[1, 0], fwd_state[2, 0])
    adjoint_in = (adj_state[0, 0], adj_state[1, 0], adj_state[2, 0])
    forward = propagate(forward_in, courant, decay_rate, strength, halo_laplace, keep_all)
    adjoint = propagate(adjoint_in, courant, decay_rate, strength, halo_laplace, keep_all)
    gradient = imaging(forward, adjoint, 1.0 / groups)
    tiled = gradient.reshape(BX, BR, BY, BC).transpose(0, 2, 1, 3).reshape(blocks_count, BR, BC)
    listed = footprint.reshape(-1)
    block_ids = jnp.arange(blocks_count, dtype=jnp.int32)
    hits = jnp.any(listed[:, None] == block_ids[None, :], axis=0).astype(jnp.float32)
    masked = tiled * hits[:, None, None]
    ordered = jnp.take(masked, owner_map.reshape(-1), axis=0)
    gradient_out = lax.psum_scatter(ordered, "emit", scatter_dimension=0, tiled=True)
    return (gradient_out, forward[STEPS + 1][None])


def solution(mesh):
    in_specs = (
        P(None, "emit", "vx", "vy"),
        P(None, "emit", "vx", "vy"),
        P("vx", "vy"),
        P("vx", "vy"),
        P("vx", "vy"),
        P("emit", "vx", "vy", None),
        P("vx", "vy", None),
    )
    out_specs = (P("emit", "vx", "vy"), P("emit", "vx", "vy"))
    return jax.shard_map(shards, mesh=mesh, in_specs=in_specs, out_specs=out_specs, check_vma=False)
```

profile of v0, /device:TPU:0, one launch (start us, length us, event | category | flops | bytes accessed | tf_op | source)
XLA Modules:
  0.0 170.7 jit_solution(18276906524478202562)
XLA Ops:
  9.2 4.9 %collective-permute-start.1 = (f32[1,256]{1,0:T(1,128)S(1)}, f32[1,256]{1,0:T(1,128)S(1)}, u32[]{:S(2)}, u32[]{:S(2)}) collective-permute-start(f32[1,256]{1,0:T(1,128)S(1)} %get-tuple-element.10), channel_id=1, source_target_pairs={{0,2},{1,3},{4,6},{5,7},{8,10},{9,11},{12,14},{13,15},{16,18},{17,... | collective-permute-start | bytes 3080 | tf_op jit(solution)/shard_map/ppermute | solution.py:18
  16.1 4.5 %collective-permute-start.17 = (f32[1,256]{1,0:T(1,128)S(1)}, f32[1,256]{1,0:T(1,128)S(1)}, u32[]{:S(2)}, u32[]{:S(2)}) collective-permute-start(f32[1,256]{1,0:T(1,128)S(1)} %get-tuple-element.8), channel_id=1, source_target_pairs={{0,2},{1,3},{4,6},{5,7},{8,10},{9,11},{12,14},{13,15},{16,18},{17,... | collective-permute-start | bytes 3080 | tf_op jit(solution)/shard_map/ppermute | solution.py:18
  24.1 1.4 collective-permute-start.3
  25.5 1.3 collective-permute-start.2
  27.0 3.2 %collective-permute-start.19 = (f32[258,1]{1,0:T(8,128)S(1)}, f32[258,1]{1,0:T(8,128)S(1)}, u32[]{:S(2)}, u32[]{:S(2)}) collective-permute-start(f32[258,1]{1,0:T(8,128)S(1)} %get-tuple-element.23), channel_id=1, source_target_pairs={{0,1},{2,3},{4,5},{6,7},{8,9},{10,11},{12,13},{14,15},{16,17},{18,... | collective-permute-start | bytes 3104 | tf_op jit(solution)/shard_map/ppermute | solution.py:18
  30.2 1.4 collective-permute-start.18
  32.0 1.3 collective-permute-start.4
  33.3 4.5 %collective-permute-start.5 = (f32[1,256]{1,0:T(1,128)S(1)}, f32[1,256]{1,0:T(1,128)S(1)}, u32[]{:S(2)}, u32[]{:S(2)}) collective-permute-start(f32[1,256]{1,0:T(1,128)S(1)} %get-tuple-element.38), channel_id=1, source_target_pairs={{0,2},{1,3},{4,6},{5,7},{8,10},{9,11},{12,14},{13,15},{16,18},{17,... | collective-permute-start | bytes 3080 | tf_op jit(solution)/shard_map/ppermute | solution.py:18
  38.2 1.3 collective-permute-start.20
  39.5 4.5 %collective-permute-start.21 = (f32[1,256]{1,0:T(1,128)S(1)}, f32[1,256]{1,0:T(1,128)S(1)}, u32[]{:S(2)}, u32[]{:S(2)}) collective-permute-start(f32[1,256]{1,0:T(1,128)S(1)} %get-tuple-element.32), channel_id=1, source_target_pairs={{0,2},{1,3},{4,6},{5,7},{8,10},{9,11},{12,14},{13,15},{16,18},{17,... | collective-permute-start | bytes 3080 | tf_op jit(solution)/shard_map/ppermute | solution.py:18
  44.2 1.9 %collective-permute-start.7 = (f32[258,1]{1,0:T(8,128)S(1)}, f32[258,1]{1,0:T(8,128)S(1)}, u32[]{:S(2)}, u32[]{:S(2)}) collective-permute-start(f32[258,1]{1,0:T(8,128)S(1)} %get-tuple-element.25), channel_id=1, source_target_pairs={{0,1},{2,3},{4,5},{6,7},{8,9},{10,11},{12,13},{14,15},{16,17},{18,... | collective-permute-start | bytes 3104 | tf_op jit(solution)/shard_map/ppermute | solution.py:18
  46.2 1.3 collective-permute-start.6
  47.6 3.0 %collective-permute-start.23 = (f32[258,1]{1,0:T(8,128)S(1)}, f32[258,1]{1,0:T(8,128)S(1)}, u32[]{:S(2)}, u32[]{:S(2)}) collective-permute-start(f32[258,1]{1,0:T(8,128)S(1)} %get-tuple-element.17), channel_id=1, source_target_pairs={{0,1},{2,3},{4,5},{6,7},{8,9},{10,11},{12,13},{14,15},{16,17},{18,... | collective-permute-start | bytes 3104 | tf_op jit(solution)/shard_map/ppermute | solution.py:18
  50.7 1.3 collective-permute-start.22
  52.3 1.3 collective-permute-start.8
  53.6 4.5 %collective-permute-start.9 = (f32[1,256]{1,0:T(1,128)S(1)}, f32[1,256]{1,0:T(1,128)S(1)}, u32[]{:S(2)}, u32[]{:S(2)}) collective-permute-start(f32[1,256]{1,0:T(1,128)S(1)} %get-tuple-element.36), channel_id=1, source_target_pairs={{0,2},{1,3},{4,6},{5,7},{8,10},{9,11},{12,14},{13,15},{16,18},{17,... | collective-permute-start | bytes 3080 | tf_op jit(solution)/shard_map/ppermute | solution.py:18
  58.5 1.3 collective-permute-start.24
  59.8 4.5 %collective-permute-start.25 = (f32[1,256]{1,0:T(1,128)S(1)}, f32[1,256]{1,0:T(1,128)S(1)}, u32[]{:S(2)}, u32[]{:S(2)}) collective-permute-start(f32[1,256]{1,0:T(1,128)S(1)} %get-tuple-element.30), channel_id=1, source_target_pairs={{0,2},{1,3},{4,6},{5,7},{8,10},{9,11},{12,14},{13,15},{16,18},{17,... | collective-permute-start | bytes 3080 | tf_op jit(solution)/shard_map/ppermute | solution.py:18
  64.5 1.9 %collective-permute-start.11 = (f32[258,1]{1,0:T(8,128)S(1)}, f32[258,1]{1,0:T(8,128)S(1)}, u32[]{:S(2)}, u32[]{:S(2)}) collective-permute-start(f32[258,1]{1,0:T(8,128)S(1)} %get-tuple-element.21), channel_id=1, source_target_pairs={{0,1},{2,3},{4,5},{6,7},{8,9},{10,11},{12,13},{14,15},{16,17},{18,... | collective-permute-start | bytes 3104 | tf_op jit(solution)/shard_map/ppermute | solution.py:18
  66.5 1.3 collective-permute-start.10
  67.9 3.0 %collective-permute-start.27 = (f32[258,1]{1,0:T(8,128)S(1)}, f32[258,1]{1,0:T(8,128)S(1)}, u32[]{:S(2)}, u32[]{:S(2)}) collective-permute-start(f32[258,1]{1,0:T(8,128)S(1)} %get-tuple-element.15), channel_id=1, source_target_pairs={{0,1},{2,3},{4,5},{6,7},{8,9},{10,11},{12,13},{14,15},{16,17},{18,... | collective-permute-start | bytes 3104 | tf_op jit(solution)/shard_map/ppermute | solution.py:18
  71.0 1.3 collective-permute-start.26
  72.8 1.3 collective-permute-start.12
  74.1 4.5 %collective-permute-start.13 = (f32[1,256]{1,0:T(1,128)S(1)}, f32[1,256]{1,0:T(1,128)S(1)}, u32[]{:S(2)}, u32[]{:S(2)}) collective-permute-start(f32[1,256]{1,0:T(1,128)S(1)} %get-tuple-element.34), channel_id=1, source_target_pairs={{0,2},{1,3},{4,6},{5,7},{8,10},{9,11},{12,14},{13,15},{16,18},{17,... | collective-permute-start | bytes 3080 | tf_op jit(solution)/shard_map/ppermute | solution.py:18
  79.3 1.3 collective-permute-start.28
  80.6 4.5 %collective-permute-start.29 = (f32[1,256]{1,0:T(1,128)S(1)}, f32[1,256]{1,0:T(1,128)S(1)}, u32[]{:S(2)}, u32[]{:S(2)}) collective-permute-start(f32[1,256]{1,0:T(1,128)S(1)} %get-tuple-element.28), channel_id=1, source_target_pairs={{0,2},{1,3},{4,6},{5,7},{8,10},{9,11},{12,14},{13,15},{16,18},{17,... | collective-permute-start | bytes 3080 | tf_op jit(solution)/shard_map/ppermute | solution.py:18
  85.3 1.9 %collective-permute-start.15 = (f32[258,1]{1,0:T(8,128)S(1)}, f32[258,1]{1,0:T(8,128)S(1)}, u32[]{:S(2)}, u32[]{:S(2)}) collective-permute-start(f32[258,1]{1,0:T(8,128)S(1)} %get-tuple-element.19), channel_id=1, source_target_pairs={{0,1},{2,3},{4,5},{6,7},{8,9},{10,11},{12,13},{14,15},{16,17},{18,... | collective-permute-start | bytes 3104 | tf_op jit(solution)/shard_map/ppermute | solution.py:18
  87.2 1.3 collective-permute-start.14
  88.7 3.0 %collective-permute-start.31 = (f32[258,1]{1,0:T(8,128)S(1)}, f32[258,1]{1,0:T(8,128)S(1)}, u32[]{:S(2)}, u32[]{:S(2)}) collective-permute-start(f32[258,1]{1,0:T(8,128)S(1)} %get-tuple-element.13), channel_id=1, source_target_pairs={{0,1},{2,3},{4,5},{6,7},{8,9},{10,11},{12,13},{14,15},{16,17},{18,... | collective-permute-start | bytes 3104 | tf_op jit(solution)/shard_map/ppermute | solution.py:18
  95.6 2.4 %fusion.38 = f32[256,256]{1,0:T(8,128)S(1)} fusion(f32[256,256]{1,0:T(8,128)S(1)} %get-tuple-element.6, f32[256,256]{1,0:T(8,128)S(1)} %multiply_add_fusion.7, f32[256,256]{1,0:T(8,128)S(1)} %get-tuple-element.4, f32[256,256]{1,0:T(8,128)S(1)} %multiply_add_fusion.5, f32[256,256]{1,0:T(8,128)S(1)} %copy-done, f32[256,256]{1,0:T(8,128)S(1)} %copy-done.1, ...), kind=kLoop, calls=%fused_computation.115 | loop fusion | flops 7929856 | bytes 3690576 | tf_op jit(solution)/shard_map/mul | solution.py:57
  99.6 1.4 broadcast_select_fusion
  103.2 60.7 %reduce-scatter.2.cloned.1.call-done = f32[4,16,128]{2,1,0:T(8,128)} async-done(((f32[32,16,128]{2,1,0:T(8,128)}), f32[4,16,128]{2,1,0:T(8,128)}) %reduce-scatter.2.cloned.1.call-update) | async-done | bytes 32784 | tf_op jit(solution)/shard_map/reduce_scatter | solution.py:74
  (111 shorter events, 18.2 us)
Async XLA Ops:
  7.2 156.7 %reduce-scatter.2.cloned.1.call-start = ((), (), s32[]{:S(2)}) async-start(), calls=%async_computation.1 | async-start | bytes 294912 | tf_op jit(solution)/shard_map/reduce_scatter | solution.py:74
  7.9 16.0 %collective-permute-start = (f32[1,256]{1,0:T(1,128)S(1)}, f32[1,256]{1,0:T(1,128)S(1)}, u32[]{:S(2)}, u32[]{:S(2)}) collective-permute-start(f32[1,256]{1,0:T(1,128)S(1)} %get-tuple-element.11), channel_id=1, source_target_pairs={{2,0},{3,1},{6,4},{7,5},{10,8},{11,9},{14,12},{15,13},{18,16},{19,... | collective-permute-start | bytes 3080 | tf_op jit(solution)/shard_map/ppermute | solution.py:21
  9.2 14.7 %collective-permute-start.1 = (f32[1,256]{1,0:T(1,128)S(1)}, f32[1,256]{1,0:T(1,128)S(1)}, u32[]{:S(2)}, u32[]{:S(2)}) collective-permute-start(f32[1,256]{1,0:T(1,128)S(1)} %get-tuple-element.10), channel_id=1, source_target_pairs={{0,2},{1,3},{4,6},{5,7},{8,10},{9,11},{12,14},{13,15},{16,18},{17,... | collective-permute-start | bytes 3080 | tf_op jit(solution)/shard_map/ppermute | solution.py:18
  14.8 12.0 %collective-permute-start.16 = (f32[1,256]{1,0:T(1,128)S(1)}, f32[1,256]{1,0:T(1,128)S(1)}, u32[]{:S(2)}, u32[]{:S(2)}) collective-permute-start(f32[1,256]{1,0:T(1,128)S(1)} %get-tuple-element.9), channel_id=1, source_target_pairs={{2,0},{3,1},{6,4},{7,5},{10,8},{11,9},{14,12},{15,13},{18,16},{19,... | collective-permute-start | bytes 3080 | tf_op jit(solution)/shard_map/ppermute | solution.py:21
  16.1 10.7 %collective-permute-start.17 = (f32[1,256]{1,0:T(1,128)S(1)}, f32[1,256]{1,0:T(1,128)S(1)}, u32[]{:S(2)}, u32[]{:S(2)}) collective-permute-start(f32[1,256]{1,0:T(1,128)S(1)} %get-tuple-element.8), channel_id=1, source_target_pairs={{0,2},{1,3},{4,6},{5,7},{8,10},{9,11},{12,14},{13,15},{16,18},{17,... | collective-permute-start | bytes 3080 | tf_op jit(solution)/shard_map/ppermute | solution.py:18
  24.1 7.6 %collective-permute-start.3 = (f32[258,1]{1,0:T(8,128)S(1)}, f32[258,1]{1,0:T(8,128)S(1)}, u32[]{:S(2)}, u32[]{:S(2)}) collective-permute-start(f32[258,1]{1,0:T(8,128)S(1)} %get-tuple-element.27), channel_id=1, source_target_pairs={{0,1},{2,3},{4,5},{6,7},{8,9},{10,11},{12,13},{14,15},{16,17},{18,... | collective-permute-start | bytes 3104 | tf_op jit(solution)/shard_map/ppermute | solution.py:18
  25.5 6.1 %collective-permute-start.2 = (f32[258,1]{1,0:T(8,128)S(1)}, f32[258,1]{1,0:T(8,128)S(1)}, u32[]{:S(2)}, u32[]{:S(2)}) collective-permute-start(f32[258,1]{1,0:T(8,128)S(1)} %get-tuple-element.26), channel_id=1, source_target_pairs={{1,0},{3,2},{5,4},{7,6},{9,8},{11,10},{13,12},{15,14},{17,16},{19,... | collective-permute-start | bytes 3104 | tf_op jit(solution)/shard_map/ppermute | solution.py:21
  27.0 10.9 %collective-permute-start.19 = (f32[258,1]{1,0:T(8,128)S(1)}, f32[258,1]{1,0:T(8,128)S(1)}, u32[]{:S(2)}, u32[]{:S(2)}) collective-permute-start(f32[258,1]{1,0:T(8,128)S(1)} %get-tuple-element.23), channel_id=1, source_target_pairs={{0,1},{2,3},{4,5},{6,7},{8,9},{10,11},{12,13},{14,15},{16,17},{18,... | collective-permute-start | bytes 3104 | tf_op jit(solution)/shard_map/ppermute | solution.py:18
  30.2 7.7 %collective-permute-start.18 = (f32[258,1]{1,0:T(8,128)S(1)}, f32[258,1]{1,0:T(8,128)S(1)}, u32[]{:S(2)}, u32[]{:S(2)}) collective-permute-start(f32[258,1]{1,0:T(8,128)S(1)} %get-tuple-element.22), channel_id=1, source_target_pairs={{1,0},{3,2},{5,4},{7,6},{9,8},{11,10},{13,12},{15,14},{17,16},{19,... | collective-permute-start | bytes 3104 | tf_op jit(solution)/shard_map/ppermute | solution.py:21
  32.0 12.1 %collective-permute-start.4 = (f32[1,256]{1,0:T(1,128)S(1)}, f32[1,256]{1,0:T(1,128)S(1)}, u32[]{:S(2)}, u32[]{:S(2)}) collective-permute-start(f32[1,256]{1,0:T(1,128)S(1)} %get-tuple-element.39), channel_id=1, source_target_pairs={{2,0},{3,1},{6,4},{7,5},{10,8},{11,9},{14,12},{15,13},{18,16},{19,... | collective-permute-start | bytes 3080 | tf_op jit(solution)/shard_map/ppermute | solution.py:21
  33.3 10.8 %collective-permute-start.5 = (f32[1,256]{1,0:T(1,128)S(1)}, f32[1,256]{1,0:T(1,128)S(1)}, u32[]{:S(2)}, u32[]{:S(2)}) collective-permute-start(f32[1,256]{1,0:T(1,128)S(1)} %get-tuple-element.38), channel_id=1, source_target_pairs={{0,2},{1,3},{4,6},{5,7},{8,10},{9,11},{12,14},{13,15},{16,18},{17,... | collective-permute-start | bytes 3080 | tf_op jit(solution)/shard_map/ppermute | solution.py:18
  38.2 9.2 %collective-permute-start.20 = (f32[1,256]{1,0:T(1,128)S(1)}, f32[1,256]{1,0:T(1,128)S(1)}, u32[]{:S(2)}, u32[]{:S(2)}) collective-permute-start(f32[1,256]{1,0:T(1,128)S(1)} %get-tuple-element.33), channel_id=1, source_target_pairs={{2,0},{3,1},{6,4},{7,5},{10,8},{11,9},{14,12},{15,13},{18,16},{19,... | collective-permute-start | bytes 3080 | tf_op jit(solution)/shard_map/ppermute | solution.py:21
  39.5 7.9 %collective-permute-start.21 = (f32[1,256]{1,0:T(1,128)S(1)}, f32[1,256]{1,0:T(1,128)S(1)}, u32[]{:S(2)}, u32[]{:S(2)}) collective-permute-start(f32[1,256]{1,0:T(1,128)S(1)} %get-tuple-element.32), channel_id=1, source_target_pairs={{0,2},{1,3},{4,6},{5,7},{8,10},{9,11},{12,14},{13,15},{16,18},{17,... | collective-permute-start | bytes 3080 | tf_op jit(solution)/shard_map/ppermute | solution.py:18
  44.2 7.7 %collective-permute-start.7 = (f32[258,1]{1,0:T(8,128)S(1)}, f32[258,1]{1,0:T(8,128)S(1)}, u32[]{:S(2)}, u32[]{:S(2)}) collective-permute-start(f32[258,1]{1,0:T(8,128)S(1)} %get-tuple-element.25), channel_id=1, source_target_pairs={{0,1},{2,3},{4,5},{6,7},{8,9},{10,11},{12,13},{14,15},{16,17},{18,... | collective-permute-start | bytes 3104 | tf_op jit(solution)/shard_map/ppermute | solution.py:18
  46.2 5.8 %collective-permute-start.6 = (f32[258,1]{1,0:T(8,128)S(1)}, f32[258,1]{1,0:T(8,128)S(1)}, u32[]{:S(2)}, u32[]{:S(2)}) collective-permute-start(f32[258,1]{1,0:T(8,128)S(1)} %get-tuple-element.24), channel_id=1, source_target_pairs={{1,0},{3,2},{5,4},{7,6},{9,8},{11,10},{13,12},{15,14},{17,16},{19,... | collective-permute-start | bytes 3104 | tf_op jit(solution)/shard_map/ppermute | solution.py:21
  47.6 10.6 %collective-permute-start.23 = (f32[258,1]{1,0:T(8,128)S(1)}, f32[258,1]{1,0:T(8,128)S(1)}, u32[]{:S(2)}, u32[]{:S(2)}) collective-permute-start(f32[258,1]{1,0:T(8,128)S(1)} %get-tuple-element.17), channel_id=1, source_target_pairs={{0,1},{2,3},{4,5},{6,7},{8,9},{10,11},{12,13},{14,15},{16,17},{18,... | collective-permute-start | bytes 3104 | tf_op jit(solution)/shard_map/ppermute | solution.py:18
  50.7 7.5 %collective-permute-start.22 = (f32[258,1]{1,0:T(8,128)S(1)}, f32[258,1]{1,0:T(8,128)S(1)}, u32[]{:S(2)}, u32[]{:S(2)}) collective-permute-start(f32[258,1]{1,0:T(8,128)S(1)} %get-tuple-element.16), channel_id=1, source_target_pairs={{1,0},{3,2},{5,4},{7,6},{9,8},{11,10},{13,12},{15,14},{17,16},{19,... | collective-permute-start | bytes 3104 | tf_op jit(solution)/shard_map/ppermute | solution.py:21
  52.3 12.0 %collective-permute-start.8 = (f32[1,256]{1,0:T(1,128)S(1)}, f32[1,256]{1,0:T(1,128)S(1)}, u32[]{:S(2)}, u32[]{:S(2)}) collective-permute-start(f32[1,256]{1,0:T(1,128)S(1)} %get-tuple-element.37), channel_id=1, source_target_pairs={{2,0},{3,1},{6,4},{7,5},{10,8},{11,9},{14,12},{15,13},{18,16},{19,... | collective-permute-start | bytes 3080 | tf_op jit(solution)/shard_map/ppermute | solution.py:21
  53.6 10.7 %collective-permute-start.9 = (f32[1,256]{1,0:T(1,128)S(1)}, f32[1,256]{1,0:T(1,128)S(1)}, u32[]{:S(2)}, u32[]{:S(2)}) collective-permute-start(f32[1,256]{1,0:T(1,128)S(1)} %get-tuple-element.36), channel_id=1, source_target_pairs={{0,2},{1,3},{4,6},{5,7},{8,10},{9,11},{12,14},{13,15},{16,18},{17,... | collective-permute-start | bytes 3080 | tf_op jit(solution)/shard_map/ppermute | solution.py:18
  58.5 9.2 %collective-permute-start.24 = (f32[1,256]{1,0:T(1,128)S(1)}, f32[1,256]{1,0:T(1,128)S(1)}, u32[]{:S(2)}, u32[]{:S(2)}) collective-permute-start(f32[1,256]{1,0:T(1,128)S(1)} %get-tuple-element.31), channel_id=1, source_target_pairs={{2,0},{3,1},{6,4},{7,5},{10,8},{11,9},{14,12},{15,13},{18,16},{19,... | collective-permute-start | bytes 3080 | tf_op jit(solution)/shard_map/ppermute | solution.py:21
  59.8 7.9 %collective-permute-start.25 = (f32[1,256]{1,0:T(1,128)S(1)}, f32[1,256]{1,0:T(1,128)S(1)}, u32[]{:S(2)}, u32[]{:S(2)}) collective-permute-start(f32[1,256]{1,0:T(1,128)S(1)} %get-tuple-element.30), channel_id=1, source_target_pairs={{0,2},{1,3},{4,6},{5,7},{8,10},{9,11},{12,14},{13,15},{16,18},{17,... | collective-permute-start | bytes 3080 | tf_op jit(solution)/shard_map/ppermute | solution.py:18
  64.5 7.7 %collective-permute-start.11 = (f32[258,1]{1,0:T(8,128)S(1)}, f32[258,1]{1,0:T(8,128)S(1)}, u32[]{:S(2)}, u32[]{:S(2)}) collective-permute-start(f32[258,1]{1,0:T(8,128)S(1)} %get-tuple-element.21), channel_id=1, source_target_pairs={{0,1},{2,3},{4,5},{6,7},{8,9},{10,11},{12,13},{14,15},{16,17},{18,... | collective-permute-start | bytes 3104 | tf_op jit(solution)/shard_map/ppermute | solution.py:18
  66.5 5.8 %collective-permute-start.10 = (f32[258,1]{1,0:T(8,128)S(1)}, f32[258,1]{1,0:T(8,128)S(1)}, u32[]{:S(2)}, u32[]{:S(2)}) collective-permute-start(f32[258,1]{1,0:T(8,128)S(1)} %get-tuple-element.20), channel_id=1, source_target_pairs={{1,0},{3,2},{5,4},{7,6},{9,8},{11,10},{13,12},{15,14},{17,16},{19,... | collective-permute-start | bytes 3104 | tf_op jit(solution)/shard_map/ppermute | solution.py:21
  67.9 10.8 %collective-permute-start.27 = (f32[258,1]{1,0:T(8,128)S(1)}, f32[258,1]{1,0:T(8,128)S(1)}, u32[]{:S(2)}, u32[]{:S(2)}) collective-permute-start(f32[258,1]{1,0:T(8,128)S(1)} %get-tuple-element.15), channel_id=1, source_target_pairs={{0,1},{2,3},{4,5},{6,7},{8,9},{10,11},{12,13},{14,15},{16,17},{18,... | collective-permute-start | bytes 3104 | tf_op jit(solution)/shard_map/ppermute | solution.py:18
  71.0 7.7 %collective-permute-start.26 = (f32[258,1]{1,0:T(8,128)S(1)}, f32[258,1]{1,0:T(8,128)S(1)}, u32[]{:S(2)}, u32[]{:S(2)}) collective-permute-start(f32[258,1]{1,0:T(8,128)S(1)} %get-tuple-element.14), channel_id=1, source_target_pairs={{1,0},{3,2},{5,4},{7,6},{9,8},{11,10},{13,12},{15,14},{17,16},{19,... | collective-permute-start | bytes 3104 | tf_op jit(solution)/shard_map/ppermute | solution.py:21
  72.8 12.3 %collective-permute-start.12 = (f32[1,256]{1,0:T(1,128)S(1)}, f32[1,256]{1,0:T(1,128)S(1)}, u32[]{:S(2)}, u32[]{:S(2)}) collective-permute-start(f32[1,256]{1,0:T(1,128)S(1)} %get-tuple-element.35), channel_id=1, source_target_pairs={{2,0},{3,1},{6,4},{7,5},{10,8},{11,9},{14,12},{15,13},{18,16},{19,... | collective-permute-start | bytes 3080 | tf_op jit(solution)/shard_map/ppermute | solution.py:21
  74.1 11.0 %collective-permute-start.13 = (f32[1,256]{1,0:T(1,128)S(1)}, f32[1,256]{1,0:T(1,128)S(1)}, u32[]{:S(2)}, u32[]{:S(2)}) collective-permute-start(f32[1,256]{1,0:T(1,128)S(1)} %get-tuple-element.34), channel_id=1, source_target_pairs={{0,2},{1,3},{4,6},{5,7},{8,10},{9,11},{12,14},{13,15},{16,18},{17,... | collective-permute-start | bytes 3080 | tf_op jit(solution)/shard_map/ppermute | solution.py:18
  79.3 9.2 %collective-permute-start.28 = (f32[1,256]{1,0:T(1,128)S(1)}, f32[1,256]{1,0:T(1,128)S(1)}, u32[]{:S(2)}, u32[]{:S(2)}) collective-permute-start(f32[1,256]{1,0:T(1,128)S(1)} %get-tuple-element.29), channel_id=1, source_target_pairs={{2,0},{3,1},{6,4},{7,5},{10,8},{11,9},{14,12},{15,13},{18,16},{19,... | collective-permute-start | bytes 3080 | tf_op jit(solution)/shard_map/ppermute | solution.py:21
  80.6 8.0 %collective-permute-start.29 = (f32[1,256]{1,0:T(1,128)S(1)}, f32[1,256]{1,0:T(1,128)S(1)}, u32[]{:S(2)}, u32[]{:S(2)}) collective-permute-start(f32[1,256]{1,0:T(1,128)S(1)} %get-tuple-element.28), channel_id=1, source_target_pairs={{0,2},{1,3},{4,6},{5,7},{8,10},{9,11},{12,14},{13,15},{16,18},{17,... | collective-permute-start | bytes 3080 | tf_op jit(solution)/shard_map/ppermute | solution.py:18
  85.3 8.9 %collective-permute-start.15 = (f32[258,1]{1,0:T(8,128)S(1)}, f32[258,1]{1,0:T(8,128)S(1)}, u32[]{:S(2)}, u32[]{:S(2)}) collective-permute-start(f32[258,1]{1,0:T(8,128)S(1)} %get-tuple-element.19), channel_id=1, source_target_pairs={{0,1},{2,3},{4,5},{6,7},{8,9},{10,11},{12,13},{14,15},{16,17},{18,... | collective-permute-start | bytes 3104 | tf_op jit(solution)/shard_map/ppermute | solution.py:18
  87.2 6.9 %collective-permute-start.14 = (f32[258,1]{1,0:T(8,128)S(1)}, f32[258,1]{1,0:T(8,128)S(1)}, u32[]{:S(2)}, u32[]{:S(2)}) collective-permute-start(f32[258,1]{1,0:T(8,128)S(1)} %get-tuple-element.18), channel_id=1, source_target_pairs={{1,0},{3,2},{5,4},{7,6},{9,8},{11,10},{13,12},{15,14},{17,16},{19,... | collective-permute-start | bytes 3104 | tf_op jit(solution)/shard_map/ppermute | solution.py:21
  88.7 5.5 %collective-permute-start.31 = (f32[258,1]{1,0:T(8,128)S(1)}, f32[258,1]{1,0:T(8,128)S(1)}, u32[]{:S(2)}, u32[]{:S(2)}) collective-permute-start(f32[258,1]{1,0:T(8,128)S(1)} %get-tuple-element.13), channel_id=1, source_target_pairs={{0,1},{2,3},{4,5},{6,7},{8,9},{10,11},{12,13},{14,15},{16,17},{18,... | collective-permute-start | bytes 3104 | tf_op jit(solution)/shard_map/ppermute | solution.py:18
  (17 other events, 100.0 us)
Sparse Core Ops, SparseCore 0:
  101.2 62.5 reduce-scatter.1
where the time goes:
time: 172 us; the launch traced here: 171 us
  starting transfers between devices  77 us (45%)
  waiting for transfers between devices  61.6 us (36%)
  between operations  14.9 us (9%)
  other arithmetic  9.41 us (5%)
  local copies, waits for them, and re-layouts  7.83 us (5%)
    reduce_scatter x1, waiting for transfers between devices, shards(): lax.psum_scatter(ordered, 'emit', scatter_dimension=0, tiled=True)  60.7 us
    ppermute x16, starting transfers between devices, with_halo(): lax.ppermute(lax.slice_in_dim(block, block.shape[dim] - width, None, axis...  56.2 us
    ppermute x16, starting transfers between devices, with_halo(): lax.ppermute(lax.slice_in_dim(block, 0, width, axis=dim), axis, backward)  20.8 us
  transfers between devices with their start and end apart: 33, of which 2 were waited for; matrix products, arithmetic and copies ran while one was open for 5% of the time, Pallas kernels for 0%

commit v1 on v0

v1 whole, which is shorter than its diff:
```python
import functools

import jax
import jax.numpy as jnp
from jax import lax
from jax.experimental import pallas as pl
from jax.experimental.pallas import tpu as pltpu
from jax.sharding import PartitionSpec as P

BR = 16
BC = 128
STEPS = 4
TOP = 16
HALO = 8
CHUNK = 16
MESH = pl.DeviceIdType.MESH


def laplace_rows(state, field, row, count, cols, lane, east_on, west_on):
    center = [state[field, j, pl.ds(row, count), :] for j in range(3)]
    east = [pltpu.roll(center[j], BC - 1, 1) for j in range(3)]
    west = [pltpu.roll(center[j], 1, 1) for j in range(3)]
    curves = []
    for j in range(cols):
        after = east[(j + 1) % 3]
        before = west[(j + 2) % 3]
        if j == 1:
            after = after * east_on
        if j == 0:
            before = before * west_on
        right = jnp.where(lane == BC - 1, after, east[j])
        left = jnp.where(lane == 0, before, west[j])
        up = state[field, j, pl.ds(row - 1, count), :]
        down = state[field, j, pl.ds(row + 1, count), :]
        curves.append((up + down) + (left + right) - 4.0 * center[j])
    return center, curves


def kernel(n_emit, n_vx, rows, fwd, adj, cour, dec, stren, listed, owner, grad, pres,
           state, saved, image, outgoing, incoming,
           load_sem, halo_send, halo_recv, block_send, block_recv, pres_sem):
    emit = lax.axis_index("emit")
    vx = lax.axis_index("vx")
    vy = lax.axis_index("vy")
    other = 1 - vy
    per = outgoing.shape[1]
    end = TOP + rows
    has_low = vx > 0
    has_high = vx < n_vx - 1

    loads = []
    for j in range(2):
        cut = pl.ds(j * BC, BC)
        place = pl.ds(TOP, rows)
        pairs = [(fwd.at[:, 0, :, cut], state.at[pl.ds(0, 3), j, place, :]),
                 (adj.at[:, 0, :, cut], state.at[pl.ds(3, 3), j, place, :])]
        for at, ref in enumerate((cour, dec, stren)):
            pairs.append((ref.at[:, cut], state.at[6 + at, j, place, :]))
        for source, target in pairs:
            copy = pltpu.make_async_copy(source, target, load_sem.at[len(loads)])
            copy.start()
            loads.append(copy)

    barrier = pltpu.get_barrier_semaphore()

    def greet(where):
        pl.semaphore_signal(barrier, inc=1, device_id=where, device_id_type=MESH)

    greet((emit, vx, other))

    @pl.when(has_low)
    def _():
        greet((emit, vx - 1, vy))
        greet((emit, vx - 1, other))

    @pl.when(has_high)
    def _():
        greet((emit, vx + 1, vy))
        greet((emit, vx + 1, other))

    for step in range(1, n_emit):
        greet((lax.rem(emit + step, n_emit), vx, vy))

    blank = jnp.zeros((HALO, BC), jnp.float32)

    @pl.when(vx == 0)
    def _():
        for field in range(9):
            for j in range(3):
                state[field, j, pl.ds(TOP - HALO, HALO), :] = blank

    @pl.when(vx == n_vx - 1)
    def _():
        for field in range(9):
            for j in range(3):
                state[field, j, pl.ds(end, HALO), :] = blank

    bits = jnp.int32(0)
    for at in range(listed.shape[-1]):
        bits = bits | lax.shift_left(jnp.int32(1), listed[0, 0, 0, at])

    for copy in loads:
        copy.wait()
    near = (vx > 0).astype(jnp.int32) + (vx < n_vx - 1).astype(jnp.int32)
    pl.semaphore_wait(barrier, n_emit + 2 * near)

    def remote(source, target, at, where):
        return pltpu.make_async_remote_copy(
            src_ref=source, dst_ref=target, send_sem=halo_send.at[at],
            recv_sem=halo_recv.at[at], device_id=where, device_id_type=MESH)

    side = remote(state.at[:, other, pl.ds(TOP, rows), :], state.at[:, 2, pl.ds(TOP, rows), :],
                  2, (emit, vx, other))
    first = pl.ds(TOP, HALO)
    last = pl.ds(end - HALO, HALO)
    above = pl.ds(TOP - HALO, HALO)
    below = pl.ds(end, HALO)
    pair = pl.ds(0, 2)

    def to_high():
        return (remote(state.at[:, pair, last, :], state.at[:, pair, above, :], 0, (emit, vx + 1, vy)),
                remote(state.at[:, other, last, :], state.at[:, 2, above, :], 3, (emit, vx + 1, other)))

    def to_low():
        return (remote(state.at[:, pair, first, :], state.at[:, pair, below, :], 1, (emit, vx - 1, vy)),
                remote(state.at[:, other, first, :], state.at[:, 2, below, :], 4, (emit, vx - 1, other)))

    @pl.when(has_high)
    def _():
        for copy in to_high():
            copy.start()

    @pl.when(has_low)
    def _():
        for copy in to_low():
            copy.start()

    side.start()

    @pl.when(has_high)
    def _():
        for copy in to_high():
            copy.wait_send()
        for copy in to_low():
            copy.wait_recv()

    @pl.when(has_low)
    def _():
        for copy in to_low():
            copy.wait_send()
        for copy in to_high():
            copy.wait_recv()

    side.wait_send()
    side.wait_recv()

    lane = lax.broadcasted_iota(jnp.int32, (CHUNK, BC), 1)
    east_on = (1 - vy).astype(jnp.float32)
    west_on = vy.astype(jnp.float32)

    def advance(base, number, row, count, cols):
        now = base + number % 2
        new = base + (number + 1) % 2
        center, curves = laplace_rows(state, now, row, count, cols, lane, east_on, west_on)
        place = pl.ds(row, count)
        seconds, fields = [], []
        for j in range(cols):
            memory = state[7, j, place, :] * state[base + 2, j, place, :] + state[8, j, place, :] * curves[j]
            second = state[6, j, place, :] * (curves[j] - memory)
            following = (2.0 * center[j] - state[new, j, place, :]) + second
            if number < STEPS:
                state[base + 2, j, place, :] = memory
            state[new, j, place, :] = following
            seconds.append(second)
            fields.append(following)
        return seconds, fields

    def step_body(number):
        def body(at, carry):
            row = TOP - HALO + at * CHUNK
            seconds, _ = advance(0, number, row, CHUNK, 3)
            _, fields = advance(3, number, row, CHUNK, 3)
            place = pl.ds(row, CHUNK)
            for j in range(2):
                if number == 1:
                    saved[0, j, place, :] = seconds[j]
                    saved[1, j, place, :] = fields[j]
                elif number == 2:
                    saved[2, j, place, :] = seconds[j]
                    saved[3, j, place, :] = fields[j]
                else:
                    saved[2, j, place, :] = (seconds[j] * saved[3, j, place, :]
                                             + fields[j] * saved[2, j, place, :])
            return carry
        return body

    for number in range(1, STEPS):
        lax.fori_loop(0, (rows + 2 * HALO) // CHUNK, step_body(number), 0)

    def last_body(at, carry):
        row = TOP + at * CHUNK
        seconds, _ = advance(0, STEPS, row, CHUNK, 2)
        _, fields = advance(3, STEPS, row, CHUNK, 2)
        place = pl.ds(row, CHUNK)
        for j in range(2):
            total = (saved[2, j, place, :] + saved[0, j, place, :] * fields[j]
                     + saved[1, j, place, :] * seconds[j])
            image[at * 2 + j] = total * (1.0 / n_emit)
        return carry

    lax.fori_loop(0, rows // CHUNK, last_body, 0)

    pres_copies = []
    for j in range(2):
        copy = pltpu.make_async_copy(state.at[(STEPS + 1) % 2, j, pl.ds(TOP, rows), :],
                                     pres.at[0, :, pl.ds(j * BC, BC)], pres_sem.at[j])
        copy.start()
        pres_copies.append(copy)

    def masked(slot):
        block = owner[0, 0, slot]
        hit = (lax.shift_right_logical(bits, block) & 1).astype(jnp.float32)
        return image[block] * hit

    def exchange(peer):
        return pltpu.make_async_remote_copy(
            src_ref=outgoing.at[peer], dst_ref=incoming.at[emit], send_sem=block_send.at[peer],
            recv_sem=block_recv.at[emit], device_id=(peer, vx, vy), device_id_type=MESH)

    for step in range(1, n_emit):
        peer = lax.rem(emit + step, n_emit)
        for at in range(per):
            outgoing[peer, at] = masked(peer * per + at)
        exchange(peer).start()

    for at in range(per):
        incoming[emit, at] = masked(emit * per + at)

    for step in range(1, n_emit):
        peer = lax.rem(emit + step, n_emit)
        pltpu.make_async_remote_copy(
            src_ref=outgoing.at[peer], dst_ref=incoming.at[peer], send_sem=block_send.at[peer],
            recv_sem=block_recv.at[peer], device_id=(peer, vx, vy), device_id_type=MESH).wait()

    for at in range(per):
        total = incoming[0, at]
        for source in range(1, n_emit):
            total = total + incoming[source, at]
        grad[at] = total
    for copy in pres_copies:
        copy.wait()


def shards(n_emit, n_vx, fwd_state, adj_state, courant, decay_rate, strength, footprint, owner_map):
    rows = fwd_state.shape[2]
    blocks = owner_map.shape[-1]
    per = blocks // n_emit
    padded = rows + 2 * TOP
    anywhere = pl.BlockSpec(memory_space=pl.ANY)
    scalars = pl.BlockSpec(memory_space=pltpu.SMEM)
    return pl.pallas_call(
        functools.partial(kernel, n_emit, n_vx, rows),
        out_shape=(jax.ShapeDtypeStruct((per, BR, BC), jnp.float32),
                   jax.ShapeDtypeStruct((1, rows, 2 * BC), jnp.float32)),
        in_specs=[anywhere] * 5 + [scalars] * 2,
        out_specs=(pl.BlockSpec(memory_space=pltpu.VMEM), anywhere),
        scratch_shapes=[
            pltpu.VMEM((9, 3, padded, BC), jnp.float32),
            pltpu.VMEM((4, 2, padded, BC), jnp.float32),
            pltpu.VMEM((blocks, BR, BC), jnp.float32),
            pltpu.VMEM((n_emit, per, BR, BC), jnp.float32),
            pltpu.VMEM((n_emit, per, BR, BC), jnp.float32),
            pltpu.SemaphoreType.DMA((10,)),
            pltpu.SemaphoreType.DMA((5,)),
            pltpu.SemaphoreType.DMA((5,)),
            pltpu.SemaphoreType.DMA((n_emit,)),
            pltpu.SemaphoreType.DMA((n_emit,)),
            pltpu.SemaphoreType.DMA((2,)),
        ],
        compiler_params=pltpu.CompilerParams(collective_id=0, has_side_effects=True),
        name="waves",
    )(fwd_state, adj_state, courant, decay_rate, strength, footprint, owner_map)


def solution(mesh):
    in_specs = (
        P(None, "emit", "vx", "vy"),
        P(None, "emit", "vx", "vy"),
        P("vx", "vy"),
        P("vx", "vy"),
        P("vx", "vy"),
        P("emit", "vx", "vy", None),
        P("vx", "vy", None),
    )
    out_specs = (P("emit", "vx", "vy"), P("emit", "vx", "vy"))
    body = functools.partial(shards, mesh.shape["emit"], mesh.shape["vx"])
    return jax.shard_map(body, mesh=mesh, in_specs=in_specs, out_specs=out_specs, check_vma=False)
```

time: 172 us -> 28.2 us (0.16)
  starting transfers between devices: 77 us -> 0 us
  waiting for transfers between devices: 61.6 us -> 0 us
  Pallas kernels: 0 us -> 24.2 us
  between operations: 14.9 us -> 0.64 us
  other arithmetic: 9.41 us -> 0 us
  local copies, waits for them, and re-layouts: 7.83 us -> 3.04 us
    ppermute x32 -> x0, starting transfers between devices: 76.9 us -> none  [the longest x16 56.2 us: with_halo(): lax.ppermute(lax.slice_in_dim(block, block.shape[dim] - width, None, axis...]
    reduce_scatter x1 -> x0, waiting for transfers between devices: 60.7 us -> none  [shards(): lax.psum_scatter(ordered, 'emit', scatter_dimension=0, tiled=True)]
    pallas_call x0 -> x1, Pallas kernels: none -> 24.2 us  [shards(): pl.pallas_call(functools.partial(kernel, n_emit, n_vx, rows), out_shape=(...]
    mul x2 -> x0, other arithmetic: 2.49 us -> none  [the longest x1 2.4 us: imaging(): return result * scale]
    add x6 -> x0, other arithmetic: 2.31 us -> none  [advance(): following = 2.0 * current - former + courant * (curve - memory)]
    slice x16 -> x0, local copies, waits for them, and re-layouts: 2.21 us -> none  [the longest x8 1.47 us: with_halo(): lax.slice_in_dim(block, block.shape[dim] - width, None, axis=dim)]
    squeeze x2 -> x0, local copies, waits for them, and re-layouts: 1.94 us -> none  [the longest x1 0.97 us: shards(): forward_in = (fwd_state[0, 0], fwd_state[1, 0], fwd_state[2, 0])]
  transfers between devices with their start and end apart: 33 -> 0, of which waited for: 2 -> 0; matrix products, arithmetic and copies ran while one was open for 5% -> 0% of each run, Pallas kernels for 0% -> 0%
where the time goes in v1:
time: 28.2 us; the launch traced here: 27.9 us
  Pallas kernels  24.2 us (86%)
  local copies, waits for them, and re-layouts  3.04 us (11%)
  between operations  0.64 us (2%)
    pallas_call x1, Pallas kernels, shards(): pl.pallas_call(functools.partial(kernel, n_emit, n_vx, rows), out_shape=(...  24.2 us
    unnamed x2, local copies, waits for them, and re-layouts  3.04 us

profile of v1, /device:TPU:0, one launch (start us, length us, event | category | flops | bytes accessed | tf_op | source)
XLA Modules:
  0.0 27.9 jit_solution(4582199486822698545)
XLA Ops:
  0.6 24.2 %waves.1 = (f32[4,16,128]{2,1,0:T(8,128)}, f32[1,256,256]{2,1,0:T(8,128)}) custom-call(f32[3,1,256,256]{3,2,1,0:T(8,128)} %fwd.1, f32[3,1,256,256]{3,2,1,0:T(8,128)} %adj.1, f32[256,256]{1,0:T(8,128)} %cour.1, f32[256,256]{1,0:T(8,128)} %dec.1, f32[256,256]{1,0:T(8,128)} %stren.1, s32[1,1,1,16]{3,2,1,0:T(1,128)} %listed.1, s32[1,1,32]{2,1,0:T(1,128)} %owner.1), custom_call_target="tpu_custom_call" | custom-call | tf_op jit(solution)/shard_map/waves/pallas_call | solution.py:261
  24.9 1.4 %copy.11 = f32[4,16,128]{2,1,0:T(8,128)} copy(f32[4,16,128]{2,1,0:T(8,128)} %get-tuple-element.4) | data formatting | bytes 65536
  26.2 1.7 %copy.12 = f32[1,256,256]{2,1,0:T(8,128)} copy(f32[1,256,256]{2,1,0:T(8,128)} %get-tuple-element.5) | data formatting | bytes 524288

commit v2 on v1

--- a/solution.py
+++ b/solution.py
@@ -37,7 +37,7 @@
 
 
 def kernel(n_emit, n_vx, rows, fwd, adj, cour, dec, stren, listed, owner, grad, pres,
-           state, saved, image, outgoing, incoming,
+           state, saved, outgoing, incoming,
            load_sem, halo_send, halo_recv, block_send, block_recv, pres_sem):
     emit = lax.axis_index("emit")
     vx = lax.axis_index("vx")
@@ -158,54 +158,101 @@
     east_on = (1 - vy).astype(jnp.float32)
     west_on = vy.astype(jnp.float32)
 
+    def update(field, base, number, cols, place):
+        center, curves, col = field
+        now_before = base + (number + 1) % 2
+        results = []
+        for j in range(cols):
+            memory = state[7, col[j], place, :] * state[base + 2, col[j], place, :] + state[8, col[j], place, :] * curves[j]
+            second = state[6, col[j], place, :] * (curves[j] - memory)
+            following = (2.0 * center[j] - state[now_before, col[j], place, :]) + second
+            results.append((memory, second, following))
+        return results
+
     def advance(base, number, row, count, cols):
-        now = base + number % 2
-        new = base + (number + 1) % 2
-        center, curves = laplace_rows(state, now, row, count, cols, lane, east_on, west_on)
-        place = pl.ds(row, count)
-        seconds, fields = [], []
-        for j in range(cols):
-            memory = state[7, j, place, :] * state[base + 2, j, place, :] + state[8, j, place, :] * curves[j]
-            second = state[6, j, place, :] * (curves[j] - memory)
-            following = (2.0 * center[j] - state[new, j, place, :]) + second
-            if number < STEPS:
-                state[base + 2, j, place, :] = memory
-            state[new, j, place, :] = following
-            seconds.append(second)
-            fields.append(following)
-        return seconds, fields
+        center, curves = laplace_rows(state, base + number % 2, row, count, cols, lane, east_on, west_on)
+        return update((center, curves, range(cols)), base, number, cols, pl.ds(row, count))
 
     def step_body(number):
+        new = (number + 1) % 2
+
         def body(at, carry):
             row = TOP - HALO + at * CHUNK
-            seconds, _ = advance(0, number, row, CHUNK, 3)
-            _, fields = advance(3, number, row, CHUNK, 3)
+            forward = advance(0, number, row, CHUNK, 3)
+            adjoint = advance(3, number, row, CHUNK, 3)
             place = pl.ds(row, CHUNK)
+            if number == 3:
+                partial = [forward[j][1] * saved[3, j, place, :] + adjoint[j][2] * saved[2, j, place, :]
+                           for j in range(2)]
+            for j in range(3):
+                for base, result in ((0, forward), (3, adjoint)):
+                    state[base + 2, j, place, :] = result[j][0]
+                    state[base + new, j, place, :] = result[j][2]
             for j in range(2):
-                if number == 1:
-                    saved[0, j, place, :] = seconds[j]
-                    saved[1, j, place, :] = fields[j]
-                elif number == 2:
-                    saved[2, j, place, :] = seconds[j]
-                    saved[3, j, place, :] = fields[j]
+                if number < 3:
+                    saved[2 * number - 2, j, place, :] = forward[j][1]
+                    saved[2 * number - 1, j, place, :] = adjoint[j][2]
                 else:
-                    saved[2, j, place, :] = (seconds[j] * saved[3, j, place, :]
-                                             + fields[j] * saved[2, j, place, :])
+                    saved[2, j, place, :] = partial[j]
             return carry
         return body
 
     for number in range(1, STEPS):
         lax.fori_loop(0, (rows + 2 * HALO) // CHUNK, step_body(number), 0)
 
+    def block_step(base, block, row):
+        now = base + STEPS % 2
+        col = block & 1
+        after_col = col + 1
+        before_col = jnp.where(col == 0, 2, 0)
+        after_on = jnp.where(col == 1, east_on, 1.0)
+        before_on = jnp.where(col == 0, west_on, 1.0)
+        place = pl.ds(row, BR)
+        center = state[now, col, place, :]
+        after = pltpu.roll(state[now, after_col, place, :], BC - 1, 1) * after_on
+        before = pltpu.roll(state[now, before_col, place, :], 1, 1) * before_on
+        right = jnp.where(lane == BC - 1, after, pltpu.roll(center, BC - 1, 1))
+        left = jnp.where(lane == 0, before, pltpu.roll(center, 1, 1))
+        up = state[now, col, pl.ds(row - 1, BR), :]
+        down = state[now, col, pl.ds(row + 1, BR), :]
+        curve = (up + down) + (left + right) - 4.0 * center
+        return update(([center], [curve], [col]), base, STEPS, 1, place)[0]
+
+    def masked(slot):
+        block = owner[0, 0, slot]
+        row = TOP + lax.shift_right_logical(block, 1) * BR
+        col = block & 1
+        hit = (lax.shift_right_logical(bits, block) & 1).astype(jnp.float32)
+        _, second, _ = block_step(0, block, row)
+        _, _, field = block_step(3, block, row)
+        place = pl.ds(row, BR)
+        total = (saved[2, col, place, :] + saved[0, col, place, :] * field
+                 + saved[1, col, place, :] * second)
+        return total * (hit * (1.0 / n_emit))
+
+    def exchange(peer, slot):
+        return pltpu.make_async_remote_copy(
+            src_ref=outgoing.at[peer], dst_ref=incoming.at[slot], send_sem=block_send.at[peer],
+            recv_sem=block_recv.at[slot], device_id=(peer, vx, vy), device_id_type=MESH)
+
+    def send_body(step, carry):
+        peer = lax.rem(emit + step, n_emit)
+        parts = [masked(peer * per + at) for at in range(per)]
+        for at in range(per):
+            outgoing[peer, at] = parts[at]
+        exchange(peer, emit).start()
+        return carry
+
+    lax.fori_loop(1, n_emit, send_body, 0)
+    parts = [masked(emit * per + at) for at in range(per)]
+    for at in range(per):
+        incoming[emit, at] = parts[at]
+
     def last_body(at, carry):
         row = TOP + at * CHUNK
-        seconds, _ = advance(0, STEPS, row, CHUNK, 2)
-        _, fields = advance(3, STEPS, row, CHUNK, 2)
-        place = pl.ds(row, CHUNK)
+        forward = advance(0, STEPS, row, CHUNK, 2)
         for j in range(2):
-            total = (saved[2, j, place, :] + saved[0, j, place, :] * fields[j]
-                     + saved[1, j, place, :] * seconds[j])
-            image[at * 2 + j] = total * (1.0 / n_emit)
+            state[(STEPS + 1) % 2, j, pl.ds(row, CHUNK), :] = forward[j][2]
         return carry
 
     lax.fori_loop(0, rows // CHUNK, last_body, 0)
@@ -217,30 +264,9 @@
         copy.start()
         pres_copies.append(copy)
 
-    def masked(slot):
-        block = owner[0, 0, slot]
-        hit = (lax.shift_right_logical(bits, block) & 1).astype(jnp.float32)
-        return image[block] * hit
-
-    def exchange(peer):
-        return pltpu.make_async_remote_copy(
-            src_ref=outgoing.at[peer], dst_ref=incoming.at[emit], send_sem=block_send.at[peer],
-            recv_sem=block_recv.at[emit], device_id=(peer, vx, vy), device_id_type=MESH)
-
     for step in range(1, n_emit):
         peer = lax.rem(emit + step, n_emit)
-        for at in range(per):
-            outgoing[peer, at] = masked(peer * per + at)
-        exchange(peer).start()
-
-    for at in range(per):
-        incoming[emit, at] = masked(emit * per + at)
-
-    for step in range(1, n_emit):
-        peer = lax.rem(emit + step, n_emit)
-        pltpu.make_async_remote_copy(
-            src_ref=outgoing.at[peer], dst_ref=incoming.at[peer], send_sem=block_send.at[peer],
-            recv_sem=block_recv.at[peer], device_id=(peer, vx, vy), device_id_type=MESH).wait()
+        exchange(peer, peer).wait()
 
     for at in range(per):
         total = incoming[0, at]
@@ -251,6 +277,15 @@
         copy.wait()
 
 
+def hand_over(found, waves, grad, pres, sem):
+    copies = [pltpu.make_async_copy(waves, pres, sem.at[0]),
+              pltpu.make_async_copy(found, grad, sem.at[1])]
+    for copy in copies:
+        copy.start()
+    for copy in copies:
+        copy.wait()
+
+
 def shards(n_emit, n_vx, fwd_state, adj_state, courant, decay_rate, strength, footprint, owner_map):
     rows = fwd_state.shape[2]
     blocks = owner_map.shape[-1]
@@ -258,7 +293,7 @@
     padded = rows + 2 * TOP
     anywhere = pl.BlockSpec(memory_space=pl.ANY)
     scalars = pl.BlockSpec(memory_space=pltpu.SMEM)
-    return pl.pallas_call(
+    found, waves = pl.pallas_call(
         functools.partial(kernel, n_emit, n_vx, rows),
         out_shape=(jax.ShapeDtypeStruct((per, BR, BC), jnp.float32),
                    jax.ShapeDtypeStruct((1, rows, 2 * BC), jnp.float32)),
@@ -267,7 +302,6 @@
         scratch_shapes=[
             pltpu.VMEM((9, 3, padded, BC), jnp.float32),
             pltpu.VMEM((4, 2, padded, BC), jnp.float32),
-            pltpu.VMEM((blocks, BR, BC), jnp.float32),
             pltpu.VMEM((n_emit, per, BR, BC), jnp.float32),
             pltpu.VMEM((n_emit, per, BR, BC), jnp.float32),
             pltpu.SemaphoreType.DMA((10,)),
@@ -280,6 +314,15 @@
         compiler_params=pltpu.CompilerParams(collective_id=0, has_side_effects=True),
         name="waves",
     )(fwd_state, adj_state, courant, decay_rate, strength, footprint, owner_map)
+    return pl.pallas_call(
+        hand_over,
+        out_shape=(jax.ShapeDtypeStruct(found.shape, jnp.float32),
+                   jax.ShapeDtypeStruct(waves.shape, jnp.float32)),
+        in_specs=[anywhere] * 2,
+        out_specs=(anywhere, anywhere),
+        scratch_shapes=[pltpu.SemaphoreType.DMA((2,))],
+        name="hand_over",
+    )(found, waves)
 
 
 def solution(mesh):

time: 28.2 us -> 34.1 us (1.21)
  Pallas kernels: 24.2 us -> 33.3 us
  local copies, waits for them, and re-layouts: 3.04 us -> 0 us
    pallas_call x0 -> x1, Pallas kernels: none -> 10.1 us  [shards(): pl.pallas_call(hand_over, out_shape=(jax.ShapeDtypeStruct(found.shape, jn...]
    unnamed x2 -> x0, local copies, waits for them, and re-layouts: 3.04 us -> none
    pallas_call x1, Pallas kernels: 24.2 us -> 23.2 us  [shards(): pl.pallas_call(functools.partial(kernel, n_emit, n_vx, rows), out_shape=(...]
where the time goes in v2:
time: 34.1 us; the launch traced here: 33.9 us
  Pallas kernels  33.3 us (98%)
  between operations  0.64 us (2%)
    pallas_call x1, Pallas kernels, shards(): pl.pallas_call(functools.partial(kernel, n_emit, n_vx, rows), out_shape=(...  23.2 us
    pallas_call x1, Pallas kernels, shards(): pl.pallas_call(hand_over, out_shape=(jax.ShapeDtypeStruct(found.shape, jn...  10.1 us

profile of v2, /device:TPU:0, one launch (start us, length us, event | category | flops | bytes accessed | tf_op | source)
XLA Modules:
  0.0 33.9 jit_solution(2725717645582134107)
XLA Ops:
  0.6 23.2 %waves.1 = (f32[4,16,128]{2,1,0:T(8,128)}, f32[1,256,256]{2,1,0:T(8,128)}) custom-call(f32[3,1,256,256]{3,2,1,0:T(8,128)} %fwd.1, f32[3,1,256,256]{3,2,1,0:T(8,128)} %adj.1, f32[256,256]{1,0:T(8,128)} %cour.1, f32[256,256]{1,0:T(8,128)} %dec.1, f32[256,256]{1,0:T(8,128)} %stren.1, s32[1,1,1,16]{3,2,1,0:T(1,128)} %listed.1, s32[1,1,32]{2,1,0:T(1,128)} %owner.1), custom_call_target="tpu_custom_call" | custom-call | tf_op jit(solution)/shard_map/waves/pallas_call | solution.py:296
  23.9 10.1 %hand_over.1 = (f32[4,16,128]{2,1,0:T(8,128)}, f32[1,256,256]{2,1,0:T(8,128)}) custom-call(f32[4,16,128]{2,1,0:T(8,128)} %get-tuple-element.4.found, f32[1,256,256]{2,1,0:T(8,128)} %get-tuple-element.5.waves), custom_call_target="tpu_custom_call" | custom-call | tf_op jit(solution)/shard_map/hand_over/pallas_call | solution.py:317

commit v3 on v2

v3 whole, which is shorter than its diff:
```python
import functools

import jax
import jax.numpy as jnp
from jax import lax
from jax.experimental import pallas as pl
from jax.experimental.pallas import tpu as pltpu
from jax.sharding import PartitionSpec as P

BR = 16
BC = 128
STEPS = 4
WIDE = 4
TOP = 16
HALO = 8
CHUNK = 32
ARRAYS = 9
MESH = pl.DeviceIdType.MESH


def lanes(count):
    return lax.broadcasted_iota(jnp.int32, (count, BC), 1)


def kernel(n_emit, n_vx, rows, fwd, adj, cour, dec, stren, listed, owner, grad, pres,
           *scratch):
    state = scratch[:ARRAYS]
    (saved, rowsend, rowrecv, colsend, colrecv, first_out, first_in, own_part, second_out, second_in,
     load_sem, halo_send, halo_recv, first_send, first_recv, second_send, second_recv,
     pres_sem) = scratch[ARRAYS:]
    courant, decay, strength = state[6:]
    emit = lax.axis_index("emit")
    vx = lax.axis_index("vx")
    vy = lax.axis_index("vy")
    other = 1 - vy
    half = n_emit // 2
    parity = lax.rem(emit, 2)
    line = emit // 2
    partner = emit + 1 - 2 * parity
    per = second_in.shape[1]
    end = TOP + rows
    has_low = vx > 0
    has_high = vx < n_vx - 1

    sources = [fwd.at[at, 0] for at in range(3)] + [adj.at[at, 0] for at in range(3)] + [cour, dec, stren]
    loads = []
    for col in (other, vy):
        cut = pl.ds(pl.multiple_of(col * BC, BC), BC)
        for at in range(ARRAYS):
            copy = pltpu.make_async_copy(sources[at].at[:, cut], state[at].at[col, pl.ds(TOP, rows), :],
                                         load_sem.at[len(loads)])
            copy.start()
            loads.append(copy)

    barrier = pltpu.get_barrier_semaphore()

    def greet(where):
        pl.semaphore_signal(barrier, inc=1, device_id=where, device_id_type=MESH)

    greet((emit, vx, other))

    @pl.when(has_low)
    def _():
        greet((emit, vx - 1, vy))
        greet((emit, vx - 1, other))

    @pl.when(has_high)
    def _():
        greet((emit, vx + 1, vy))
        greet((emit, vx + 1, other))

    greet((partner, vx, vy))
    for step in range(1, half):
        greet((2 * lax.rem(line + step, half) + parity, vx, vy))

    @pl.when(vx == 0)
    def _():
        rowrecv[0] = jnp.zeros(rowrecv.shape[1:], jnp.float32)
        colrecv[pl.ds(0, HALO), :] = jnp.zeros((HALO, BC), jnp.float32)

    @pl.when(vx == n_vx - 1)
    def _():
        rowrecv[1] = jnp.zeros(rowrecv.shape[1:], jnp.float32)
        colrecv[pl.ds(HALO + rows, HALO), :] = jnp.zeros((HALO, BC), jnp.float32)

    bits = jnp.int32(0)
    for at in range(listed.shape[-1]):
        bits = bits | lax.shift_left(jnp.int32(1), listed[0, 0, 0, at])

    for copy in loads[:ARRAYS]:
        copy.wait()
    base = other * (BC - WIDE)
    group = lax.rem(lanes(CHUNK) + (BC - base), BC) // WIDE

    def pack(at, carry):
        row = at * CHUNK
        packed = state[0][other, pl.ds(TOP + row, CHUNK), :]
        for which in range(1, ARRAYS):
            moved = pltpu.roll(state[which][other, pl.ds(TOP + row, CHUNK), :], WIDE * which, 1)
            packed = jnp.where(group == which, moved, packed)
        colsend[pl.ds(row, CHUNK), :] = packed
        return carry

    lax.fori_loop(0, rows // CHUNK, pack, 0)
    for copy in loads[ARRAYS:]:
        copy.wait()
    for which in range(ARRAYS):
        for col in range(2):
            place = pl.ds(WIDE * which, WIDE)
            rowsend[0, col, place, :] = state[which][col, pl.ds(TOP, WIDE), :]
            rowsend[1, col, place, :] = state[which][col, pl.ds(end - WIDE, WIDE), :]

    near = (vx > 0).astype(jnp.int32) + (vx < n_vx - 1).astype(jnp.int32)
    pl.semaphore_wait(barrier, half + 1 + 2 * near)

    def remote(source, target, at, where):
        return pltpu.make_async_remote_copy(
            src_ref=source, dst_ref=target, send_sem=halo_send.at[at],
            recv_sem=halo_recv.at[at], device_id=where, device_id_type=MESH)

    side = remote(colsend, colrecv.at[pl.ds(HALO, rows), :], 2, (emit, vx, other))

    def to_high():
        return (remote(rowsend.at[1], rowrecv.at[0], 0, (emit, vx + 1, vy)),
                remote(colsend.at[pl.ds(rows - HALO, HALO), :], colrecv.at[pl.ds(0, HALO), :], 3,
                       (emit, vx + 1, other)))

    def to_low():
        return (remote(rowsend.at[0], rowrecv.at[1], 1, (emit, vx - 1, vy)),
                remote(colsend.at[pl.ds(0, HALO), :], colrecv.at[pl.ds(HALO + rows, HALO), :], 4,
                       (emit, vx - 1, other)))

    @pl.when(has_high)
    def _():
        for copy in to_high():
            copy.start()

    @pl.when(has_low)
    def _():
        for copy in to_low():
            copy.start()

    side.start()

    @pl.when(has_high)
    def _():
        for copy in to_low():
            copy.wait_recv()

    @pl.when(has_low)
    def _():
        for copy in to_high():
            copy.wait_recv()

    side.wait_recv()

    unpack_rows = (rows + 2 * HALO) // 2

    def unpack(at, carry):
        packed = colrecv[pl.ds(at * unpack_rows, unpack_rows), :]
        for which in range(ARRAYS):
            moved = packed if which == 0 else pltpu.roll(packed, BC - WIDE * which, 1)
            state[which][2, pl.ds(TOP - HALO + at * unpack_rows, unpack_rows), :] = moved
        return carry

    lax.fori_loop(0, 2, unpack, 0)
    for which in range(ARRAYS):
        for col in range(2):
            place = pl.ds(WIDE * which, WIDE)
            state[which][col, pl.ds(TOP - WIDE, WIDE), :] = rowrecv[0, col, place, :]
            state[which][col, pl.ds(end, WIDE), :] = rowrecv[1, col, place, :]

    east_on = (1 - vy).astype(jnp.float32)
    west_on = vy.astype(jnp.float32)

    def laplace_rows(field, row, count, cols):
        lane = lanes(count)
        center = [field[j, pl.ds(row, count), :] for j in range(3)]
        east = [pltpu.roll(center[j], BC - 1, 1) for j in range(3)]
        west = [pltpu.roll(center[j], 1, 1) for j in range(3)]
        curves = []
        for j in range(cols):
            after = east[(j + 1) % 3]
            before = west[(j + 2) % 3]
            if j == 1:
                after = after * east_on
            if j == 0:
                before = before * west_on
            right = jnp.where(lane == BC - 1, after, east[j])
            left = jnp.where(lane == 0, before, west[j])
            up = field[j, pl.ds(row - 1, count), :]
            down = field[j, pl.ds(row + 1, count), :]
            curves.append((up + down) + (left + right) - 4.0 * center[j])
        return center, curves

    def update(base, number, col, place, center, curve):
        memory = decay[col, place, :] * state[base + 2][col, place, :] + strength[col, place, :] * curve
        second = courant[col, place, :] * (curve - memory)
        following = (2.0 * center - state[base + (number + 1) % 2][col, place, :]) + second
        return memory, second, following

    def advance(base, number, row, count, cols):
        center, curves = laplace_rows(state[base + number % 2], row, count, cols)
        return [update(base, number, j, pl.ds(row, count), center[j], curves[j]) for j in range(cols)]

    def step_rows(number, row, count, keep):
        place = pl.ds(row, count)
        new = (number + 1) % 2
        results = []
        for base in (0, 3):
            result = advance(base, number, row, count, 3)
            for j in range(3):
                state[base + 2][j, place, :] = result[j][0]
                state[base + new][j, place, :] = result[j][2]
            results.append(result)
        if not keep:
            return
        forward, adjoint = results
        for j in range(2):
            if number < 3:
                saved[2 * number - 2, j, place, :] = forward[j][1]
                saved[2 * number - 1, j, place, :] = adjoint[j][2]
            else:
                saved[2, j, place, :] = (forward[j][1] * saved[3, j, place, :]
                                         + adjoint[j][2] * saved[2, j, place, :])

    for number in range(1, STEPS):
        def body(at, carry, number=number):
            step_rows(number, TOP + at * CHUNK, CHUNK, True)
            return carry

        lax.fori_loop(0, rows // CHUNK, body, 0)
        step_rows(number, TOP - HALO, HALO, False)
        step_rows(number, end, HALO, False)

    lane = lanes(BR)

    def block_step(base, block, row):
        field = state[base + STEPS % 2]
        col = block & 1
        before_col = jnp.where(col == 0, 2, 0)
        after_on = jnp.where(col == 1, east_on, 1.0)
        before_on = jnp.where(col == 0, west_on, 1.0)
        place = pl.ds(row, BR)
        center = field[col, place, :]
        after = pltpu.roll(field[col + 1, place, :], BC - 1, 1) * after_on
        before = pltpu.roll(field[before_col, place, :], 1, 1) * before_on
        right = jnp.where(lane == BC - 1, after, pltpu.roll(center, BC - 1, 1))
        left = jnp.where(lane == 0, before, pltpu.roll(center, 1, 1))
        up = field[col, pl.ds(row - 1, BR), :]
        down = field[col, pl.ds(row + 1, BR), :]
        curve = (up + down) + (left + right) - 4.0 * center
        return update(base, STEPS, col, place, center, curve)

    def masked(slot):
        block = owner[0, 0, slot]
        row = TOP + lax.shift_right_logical(block, 1) * BR
        col = block & 1
        hit = (lax.shift_right_logical(bits, block) & 1).astype(jnp.float32)
        _, second, _ = block_step(0, block, row)
        _, _, field = block_step(3, block, row)
        place = pl.ds(row, BR)
        total = (saved[2, col, place, :] + saved[0, col, place, :] * field
                 + saved[1, col, place, :] * second)
        return total * (hit * (1.0 / n_emit))

    def to_partner(at):
        return pltpu.make_async_remote_copy(
            src_ref=first_out.at[at], dst_ref=first_in.at[at], send_sem=first_send.at[at],
            recv_sem=first_recv.at[at], device_id=(partner, vx, vy), device_id_type=MESH)

    def to_owner(at, slot):
        return pltpu.make_async_remote_copy(
            src_ref=second_out.at[at], dst_ref=second_in.at[slot], send_sem=second_send.at[at],
            recv_sem=second_recv.at[slot], device_id=(2 * at + parity, vx, vy), device_id_type=MESH)

    offsets = [half // 2 + at for at in range(half - half // 2)] + list(range(1, half // 2)) + [0]
    order = [lax.rem(line + offset, half) for offset in offsets]

    for at in order:
        parts = [masked((2 * at + 1 - parity) * per + slot) for slot in range(per)]
        for slot in range(per):
            first_out[at, slot] = parts[slot]
        to_partner(at).start()
    for at in order:
        parts = [masked((2 * at + parity) * per + slot) for slot in range(per)]
        for slot in range(per):
            own_part[at, slot] = parts[slot]
    for at in order[:-1]:
        to_partner(at).wait_recv()
        second_out[at] = own_part[at] + first_in[at]
        to_owner(at, line).start()
    to_partner(line).wait_recv()
    second_in[line] = own_part[line] + first_in[line]

    def last_body(at, carry):
        row = TOP + at * CHUNK
        forward = advance(0, STEPS, row, CHUNK, 2)
        for j in range(2):
            state[(STEPS + 1) % 2][j, pl.ds(row, CHUNK), :] = forward[j][2]
        return carry

    lax.fori_loop(0, rows // CHUNK, last_body, 0)

    pres_copies = []
    for j in range(2):
        copy = pltpu.make_async_copy(state[(STEPS + 1) % 2].at[j, pl.ds(TOP, rows), :],
                                     pres.at[0, :, pl.ds(j * BC, BC)], pres_sem.at[j])
        copy.start()
        pres_copies.append(copy)

    side.wait_send()

    @pl.when(has_high)
    def _():
        for copy in to_high():
            copy.wait_send()

    @pl.when(has_low)
    def _():
        for copy in to_low():
            copy.wait_send()

    for at in range(half):
        to_partner(at).wait_send()
    for at in order[:-1]:
        to_owner(at, at).wait()
    total = second_in[0]
    for at in range(1, half):
        total = total + second_in[at]
    grad[...] = total
    for copy in pres_copies:
        copy.wait()


def hand_over(found, waves, grad, pres, found_here, waves_here, sem):
    parts = 4
    rows = waves.shape[1] // parts
    steps = [(found, found_here, grad)]
    for at in range(parts):
        place = pl.ds(at * rows, rows)
        steps.append((waves.at[:, place, :], waves_here.at[:, place, :], pres.at[:, place, :]))
    taken = [pltpu.make_async_copy(source, here, sem.at[0, at]) for at, (source, here, _) in enumerate(steps)]
    given = [pltpu.make_async_copy(here, target, sem.at[1, at]) for at, (_, here, target) in enumerate(steps)]
    for copy in taken:
        copy.start()
    for into, out in zip(taken, given):
        into.wait()
        out.start()
    for copy in given:
        copy.wait()


def shards(n_emit, n_vx, fwd_state, adj_state, courant, decay_rate, strength, footprint, owner_map):
    rows = fwd_state.shape[2]
    blocks = owner_map.shape[-1]
    per = blocks // n_emit
    half = n_emit // 2
    padded = rows + 2 * TOP
    anywhere = pl.BlockSpec(memory_space=pl.ANY)
    scalars = pl.BlockSpec(memory_space=pltpu.SMEM)

    def blocks_of(count):
        return pltpu.VMEM((count, per, BR, BC), jnp.float32)

    found, waves = pl.pallas_call(
        functools.partial(kernel, n_emit, n_vx, rows),
        out_shape=(jax.ShapeDtypeStruct((per, BR, BC), jnp.float32),
                   jax.ShapeDtypeStruct((1, rows, 2 * BC), jnp.float32)),
        in_specs=[anywhere] * 5 + [scalars] * 2,
        out_specs=(pl.BlockSpec(memory_space=pltpu.VMEM), anywhere),
        scratch_shapes=[pltpu.VMEM((3, padded, BC), jnp.float32)] * ARRAYS + [
            pltpu.VMEM((4, 2, padded, BC), jnp.float32),
            pltpu.VMEM((2, 2, 40, BC), jnp.float32),
            pltpu.VMEM((2, 2, 40, BC), jnp.float32),
            pltpu.VMEM((rows, BC), jnp.float32),
            pltpu.VMEM((rows + 2 * HALO, BC), jnp.float32),
        ] + [blocks_of(half)] * 5 + [
            pltpu.SemaphoreType.DMA((2 * ARRAYS,)),
            pltpu.SemaphoreType.DMA((5,)),
            pltpu.SemaphoreType.DMA((5,)),
            pltpu.SemaphoreType.DMA((half,)),
            pltpu.SemaphoreType.DMA((half,)),
            pltpu.SemaphoreType.DMA((half,)),
            pltpu.SemaphoreType.DMA((half,)),
            pltpu.SemaphoreType.DMA((2,)),
        ],
        compiler_params=pltpu.CompilerParams(collective_id=0, has_side_effects=True),
        name="waves",
    )(fwd_state, adj_state, courant, decay_rate, strength, footprint, owner_map)
    return pl.pallas_call(
        hand_over,
        out_shape=(jax.ShapeDtypeStruct(found.shape, jnp.float32),
                   jax.ShapeDtypeStruct(waves.shape, jnp.float32)),
        in_specs=[anywhere] * 2,
        out_specs=(anywhere, anywhere),
        scratch_shapes=[pltpu.VMEM(found.shape, jnp.float32), pltpu.VMEM(waves.shape, jnp.float32),
                        pltpu.SemaphoreType.DMA((2, 5))],
        name="hand_over",
    )(found, waves)


def solution(mesh):
    in_specs = (
        P(None, "emit", "vx", "vy"),
        P(None, "emit", "vx", "vy"),
        P("vx", "vy"),
        P("vx", "vy"),
        P("vx", "vy"),
        P("emit", "vx", "vy", None),
        P("vx", "vy", None),
    )
    out_specs = (P("emit", "vx", "vy"), P("emit", "vx", "vy"))
    body = functools.partial(shards, mesh.shape["emit"], mesh.shape["vx"])
    return jax.shard_map(body, mesh=mesh, in_specs=in_specs, out_specs=out_specs, check_vma=False)
```

time: 34.1 us -> 26 us (0.76)
  Pallas kernels: 33.3 us -> 25.2 us
    pallas_call x1, Pallas kernels: 10.1 us -> 1.67 us  [shards(): pl.pallas_call(hand_over, out_shape=(jax.ShapeDtypeStruct(found.shape, jn...]
where the time goes in v3:
time: 26 us; the launch traced here: 25.8 us
  Pallas kernels  25.2 us (97%)
  between operations  0.64 us (2%)
    pallas_call x1, Pallas kernels, shards(): pl.pallas_call(functools.partial(kernel, n_emit, n_vx, rows), out_shape=(...  23.5 us
    pallas_call x1, Pallas kernels, shards(): pl.pallas_call(hand_over, out_shape=(jax.ShapeDtypeStruct(found.shape, jn...  1.67 us

profile of v3, /device:TPU:0, one launch (start us, length us, event | category | flops | bytes accessed | tf_op | source)
XLA Modules:
  0.0 25.8 jit_solution(11742379154753354601)
XLA Ops:
  0.6 23.5 %waves.1 = (f32[4,16,128]{2,1,0:T(8,128)}, f32[1,256,256]{2,1,0:T(8,128)}) custom-call(f32[3,1,256,256]{3,2,1,0:T(8,128)} %fwd.1, f32[3,1,256,256]{3,2,1,0:T(8,128)} %adj.1, f32[256,256]{1,0:T(8,128)} %cour.1, f32[256,256]{1,0:T(8,128)} %dec.1, f32[256,256]{1,0:T(8,128)} %stren.1, s32[1,1,1,16]{3,2,1,0:T(1,128)} %listed.1, s32[1,1,32]{2,1,0:T(1,128)} %owner.1), custom_call_target="tpu_custom_call" | custom-call | tf_op jit(solution)/shard_map/waves/pallas_call | solution.py:366
  24.2 1.7 %hand_over.1 = (f32[4,16,128]{2,1,0:T(8,128)}, f32[1,256,256]{2,1,0:T(8,128)}) custom-call(f32[4,16,128]{2,1,0:T(8,128)} %get-tuple-element.4.found, f32[1,256,256]{2,1,0:T(8,128)} %get-tuple-element.5.waves), custom_call_target="tpu_custom_call" | custom-call | tf_op jit(solution)/shard_map/hand_over/pallas_call | solution.py:391

commit v4 on v3

--- a/solution.py
+++ b/solution.py
@@ -22,12 +22,11 @@
     return lax.broadcasted_iota(jnp.int32, (count, BC), 1)
 
 
-def kernel(n_emit, n_vx, rows, fwd, adj, cour, dec, stren, listed, owner, grad, pres,
+def kernel(n_emit, n_vx, rows, fwd, adj, cour, dec, stren, listed_far, owner_far, grad, pres,
            *scratch):
     state = scratch[:ARRAYS]
-    (saved, rowsend, rowrecv, colsend, colrecv, first_out, first_in, own_part, second_out, second_in,
-     load_sem, halo_send, halo_recv, first_send, first_recv, second_send, second_recv,
-     pres_sem) = scratch[ARRAYS:]
+    (saved, rowsend, rowrecv, colsend, colrecv, outgoing, incoming, listed, owner,
+     load_sem, halo_send, halo_recv, block_send, block_recv, pres_sem, list_sem) = scratch[ARRAYS:]
     courant, decay, strength = state[6:]
     emit = lax.axis_index("emit")
     vx = lax.axis_index("vx")
@@ -37,7 +36,7 @@
     parity = lax.rem(emit, 2)
     line = emit // 2
     partner = emit + 1 - 2 * parity
-    per = second_in.shape[1]
+    per = incoming.shape[1]
     end = TOP + rows
     has_low = vx > 0
     has_high = vx < n_vx - 1
@@ -69,9 +68,13 @@
         greet((emit, vx + 1, vy))
         greet((emit, vx + 1, other))
 
-    greet((partner, vx, vy))
-    for step in range(1, half):
-        greet((2 * lax.rem(line + step, half) + parity, vx, vy))
+    for step in range(1, n_emit):
+        greet((lax.rem(emit + step, n_emit), vx, vy))
+
+    lists = [pltpu.make_async_copy(listed_far, listed, list_sem.at[0]),
+             pltpu.make_async_copy(owner_far, owner, list_sem.at[1])]
+    for copy in lists:
+        copy.start()
 
     @pl.when(vx == 0)
     def _():
@@ -82,10 +85,6 @@
     def _():
         rowrecv[1] = jnp.zeros(rowrecv.shape[1:], jnp.float32)
         colrecv[pl.ds(HALO + rows, HALO), :] = jnp.zeros((HALO, BC), jnp.float32)
-
-    bits = jnp.int32(0)
-    for at in range(listed.shape[-1]):
-        bits = bits | lax.shift_left(jnp.int32(1), listed[0, 0, 0, at])
 
     for copy in loads[:ARRAYS]:
         copy.wait()
@@ -111,7 +110,7 @@
             rowsend[1, col, place, :] = state[which][col, pl.ds(end - WIDE, WIDE), :]
 
     near = (vx > 0).astype(jnp.int32) + (vx < n_vx - 1).astype(jnp.int32)
-    pl.semaphore_wait(barrier, half + 1 + 2 * near)
+    pl.semaphore_wait(barrier, n_emit + 2 * near)
 
     def remote(source, target, at, where):
         return pltpu.make_async_remote_copy(
@@ -141,6 +140,12 @@
             copy.start()
 
     side.start()
+
+    for copy in lists:
+        copy.wait()
+    bits = jnp.int32(0)
+    for at in range(listed.shape[-1]):
+        bits = bits | lax.shift_left(jnp.int32(1), listed[0, 0, 0, at])
 
     @pl.when(has_high)
     def _():
@@ -264,34 +269,22 @@
                  + saved[1, col, place, :] * second)
         return total * (hit * (1.0 / n_emit))
 
-    def to_partner(at):
+    def exchange(peer, slot):
         return pltpu.make_async_remote_copy(
-            src_ref=first_out.at[at], dst_ref=first_in.at[at], send_sem=first_send.at[at],
-            recv_sem=first_recv.at[at], device_id=(partner, vx, vy), device_id_type=MESH)
-
-    def to_owner(at, slot):
-        return pltpu.make_async_remote_copy(
-            src_ref=second_out.at[at], dst_ref=second_in.at[slot], send_sem=second_send.at[at],
-            recv_sem=second_recv.at[slot], device_id=(2 * at + parity, vx, vy), device_id_type=MESH)
-
-    offsets = [half // 2 + at for at in range(half - half // 2)] + list(range(1, half // 2)) + [0]
-    order = [lax.rem(line + offset, half) for offset in offsets]
-
-    for at in order:
-        parts = [masked((2 * at + 1 - parity) * per + slot) for slot in range(per)]
+            src_ref=outgoing.at[peer], dst_ref=incoming.at[slot], send_sem=block_send.at[peer],
+            recv_sem=block_recv.at[slot], device_id=(peer, vx, vy), device_id_type=MESH)
+
+    offsets = [half // 2 + at for at in range(half - half // 2)] + list(range(1, half // 2))
+    peers = [2 * lax.rem(line + offset, half) + side_of for offset in offsets
+             for side_of in (parity, 1 - parity)] + [partner]
+    for peer in peers:
+        parts = [masked(peer * per + slot) for slot in range(per)]
         for slot in range(per):
-            first_out[at, slot] = parts[slot]
-        to_partner(at).start()
-    for at in order:
-        parts = [masked((2 * at + parity) * per + slot) for slot in range(per)]
-        for slot in range(per):
-            own_part[at, slot] = parts[slot]
-    for at in order[:-1]:
-        to_partner(at).wait_recv()
-        second_out[at] = own_part[at] + first_in[at]
-        to_owner(at, line).start()
-    to_partner(line).wait_recv()
-    second_in[line] = own_part[line] + first_in[line]
+            outgoing[peer, slot] = parts[slot]
+        exchange(peer, emit).start()
+    parts = [masked(emit * per + slot) for slot in range(per)]
+    for slot in range(per):
+        incoming[emit, slot] = parts[slot]
 
     def last_body(at, carry):
         row = TOP + at * CHUNK
@@ -321,13 +314,11 @@
         for copy in to_low():
             copy.wait_send()
 
-    for at in range(half):
-        to_partner(at).wait_send()
-    for at in order[:-1]:
-        to_owner(at, at).wait()
-    total = second_in[0]
-    for at in range(1, half):
-        total = total + second_in[at]
+    for peer in peers[::-1]:
+        exchange(peer, peer).wait()
+    total = incoming[0]
+    for at in range(1, n_emit):
+        total = total + incoming[at]
     grad[...] = total
     for copy in pres_copies:
         copy.wait()
@@ -355,10 +346,9 @@
     rows = fwd_state.shape[2]
     blocks = owner_map.shape[-1]
     per = blocks // n_emit
-    half = n_emit // 2
     padded = rows + 2 * TOP
     anywhere = pl.BlockSpec(memory_space=pl.ANY)
-    scalars = pl.BlockSpec(memory_space=pltpu.SMEM)
+    far = pl.BlockSpec(memory_space=pltpu.HBM)
 
     def blocks_of(count):
         return pltpu.VMEM((count, per, BR, BC), jnp.float32)
@@ -367,7 +357,7 @@
         functools.partial(kernel, n_emit, n_vx, rows),
         out_shape=(jax.ShapeDtypeStruct((per, BR, BC), jnp.float32),
                    jax.ShapeDtypeStruct((1, rows, 2 * BC), jnp.float32)),
-        in_specs=[anywhere] * 5 + [scalars] * 2,
+        in_specs=[far] * 7,
         out_specs=(pl.BlockSpec(memory_space=pltpu.VMEM), anywhere),
         scratch_shapes=[pltpu.VMEM((3, padded, BC), jnp.float32)] * ARRAYS + [
             pltpu.VMEM((4, 2, padded, BC), jnp.float32),
@@ -375,14 +365,15 @@
             pltpu.VMEM((2, 2, 40, BC), jnp.float32),
             pltpu.VMEM((rows, BC), jnp.float32),
             pltpu.VMEM((rows + 2 * HALO, BC), jnp.float32),
-        ] + [blocks_of(half)] * 5 + [
+        ] + [blocks_of(n_emit)] * 2 + [
+            pltpu.SMEM(footprint.shape, jnp.int32),
+            pltpu.SMEM(owner_map.shape, jnp.int32),
             pltpu.SemaphoreType.DMA((2 * ARRAYS,)),
             pltpu.SemaphoreType.DMA((5,)),
             pltpu.SemaphoreType.DMA((5,)),
-            pltpu.SemaphoreType.DMA((half,)),
-            pltpu.SemaphoreType.DMA((half,)),
-            pltpu.SemaphoreType.DMA((half,)),
-            pltpu.SemaphoreType.DMA((half,)),
+            pltpu.SemaphoreType.DMA((n_emit,)),
+            pltpu.SemaphoreType.DMA((n_emit,)),
+            pltpu.SemaphoreType.DMA((2,)),
             pltpu.SemaphoreType.DMA((2,)),
         ],
         compiler_params=pltpu.CompilerParams(collective_id=0, has_side_effects=True),

time: 26 us -> 24.7 us (0.950)
  Pallas kernels: 25.2 us -> 23.9 us
    pallas_call x1, Pallas kernels: 23.5 us -> 22.2 us  [shards(): pl.pallas_call(functools.partial(kernel, n_emit, n_vx, rows), out_shape=(...]
where the time goes in v4:
time: 24.7 us; the launch traced here: 24.5 us
  Pallas kernels  23.9 us (97%)
  between operations  0.64 us (3%)
    pallas_call x1, Pallas kernels, shards(): pl.pallas_call(functools.partial(kernel, n_emit, n_vx, rows), out_shape=(...  22.2 us
    pallas_call x1, Pallas kernels, shards(): pl.pallas_call(hand_over, out_shape=(jax.ShapeDtypeStruct(found.shape, jn...  1.67 us

profile of v4, /device:TPU:0, one launch (start us, length us, event | category | flops | bytes accessed | tf_op | source)
XLA Modules:
  0.0 24.5 jit_solution(17818521691763505238)
XLA Ops:
  0.6 22.2 %waves.1 = (f32[4,16,128]{2,1,0:T(8,128)}, f32[1,256,256]{2,1,0:T(8,128)}) custom-call(f32[3,1,256,256]{3,2,1,0:T(8,128)} %fwd.1, f32[3,1,256,256]{3,2,1,0:T(8,128)} %adj.1, f32[256,256]{1,0:T(8,128)} %cour.1, f32[256,256]{1,0:T(8,128)} %dec.1, f32[256,256]{1,0:T(8,128)} %stren.1, s32[1,1,1,16]{3,2,1,0:T(1,128)} %listed_far.1, s32[1,1,32]{2,1,0:T(1,128)} %owner_far.1), custom_call_target="tpu_custom_call" | custom-call | tf_op jit(solution)/shard_map/waves/pallas_call | solution.py:356
  22.9 1.7 %hand_over.1 = (f32[4,16,128]{2,1,0:T(8,128)}, f32[1,256,256]{2,1,0:T(8,128)}) custom-call(f32[4,16,128]{2,1,0:T(8,128)} %get-tuple-element.4.found, f32[1,256,256]{2,1,0:T(8,128)} %get-tuple-element.5.waves), custom_call_target="tpu_custom_call" | custom-call | tf_op jit(solution)/shard_map/hand_over/pallas_call | solution.py:382

commit v5 on v3

--- a/solution.py
+++ b/solution.py
@@ -22,12 +22,12 @@
     return lax.broadcasted_iota(jnp.int32, (count, BC), 1)
 
 
-def kernel(n_emit, n_vx, rows, fwd, adj, cour, dec, stren, listed, owner, grad, pres,
+def kernel(n_emit, n_vx, rows, fwd, adj, cour, dec, stren, listed_far, owner_far, grad, pres,
            *scratch):
     state = scratch[:ARRAYS]
-    (saved, rowsend, rowrecv, colsend, colrecv, first_out, first_in, own_part, second_out, second_in,
-     load_sem, halo_send, halo_recv, first_send, first_recv, second_send, second_recv,
-     pres_sem) = scratch[ARRAYS:]
+    (saved, rowsend, rowrecv, colsend, colrecv, outgoing, incoming, first_out, first_in, own_part, second_out, second_in,
+     listed, owner, load_sem, halo_send, halo_recv, block_send, block_recv, first_send, first_recv,
+     second_send, second_recv, pres_sem, list_sem) = scratch[ARRAYS:]
     courant, decay, strength = state[6:]
     emit = lax.axis_index("emit")
     vx = lax.axis_index("vx")
@@ -37,7 +37,8 @@
     parity = lax.rem(emit, 2)
     line = emit // 2
     partner = emit + 1 - 2 * parity
-    per = second_in.shape[1]
+    joint = second_in.shape[1]
+    per = grad.shape[0]
     end = TOP + rows
     has_low = vx > 0
     has_high = vx < n_vx - 1
@@ -69,9 +70,13 @@
         greet((emit, vx + 1, vy))
         greet((emit, vx + 1, other))
 
-    greet((partner, vx, vy))
-    for step in range(1, half):
-        greet((2 * lax.rem(line + step, half) + parity, vx, vy))
+    for step in range(1, n_emit):
+        greet((lax.rem(emit + step, n_emit), vx, vy))
+
+    lists = [pltpu.make_async_copy(listed_far, listed, list_sem.at[0]),
+             pltpu.make_async_copy(owner_far, owner, list_sem.at[1])]
+    for copy in lists:
+        copy.start()
 
     @pl.when(vx == 0)
     def _():
@@ -82,10 +87,6 @@
     def _():
         rowrecv[1] = jnp.zeros(rowrecv.shape[1:], jnp.float32)
         colrecv[pl.ds(HALO + rows, HALO), :] = jnp.zeros((HALO, BC), jnp.float32)
-
-    bits = jnp.int32(0)
-    for at in range(listed.shape[-1]):
-        bits = bits | lax.shift_left(jnp.int32(1), listed[0, 0, 0, at])
 
     for copy in loads[:ARRAYS]:
         copy.wait()
@@ -102,6 +103,18 @@
         return carry
 
     lax.fori_loop(0, rows // CHUNK, pack, 0)
+    near = (vx > 0).astype(jnp.int32) + (vx < n_vx - 1).astype(jnp.int32)
+    pl.semaphore_wait(barrier, n_emit + 2 * near)
+
+    def remote(source, target, at, where):
+        return pltpu.make_async_remote_copy(
+            src_ref=source, dst_ref=target, send_sem=halo_send.at[at],
+            recv_sem=halo_recv.at[at], device_id=where, device_id_type=MESH)
+
+    side = remote(colsend, colrecv.at[pl.ds(HALO, rows), :], 2, (emit, vx, other))
+
+    side.start()
+
     for copy in loads[ARRAYS:]:
         copy.wait()
     for which in range(ARRAYS):
@@ -110,16 +123,6 @@
             rowsend[0, col, place, :] = state[which][col, pl.ds(TOP, WIDE), :]
             rowsend[1, col, place, :] = state[which][col, pl.ds(end - WIDE, WIDE), :]
 
-    near = (vx > 0).astype(jnp.int32) + (vx < n_vx - 1).astype(jnp.int32)
-    pl.semaphore_wait(barrier, half + 1 + 2 * near)
-
-    def remote(source, target, at, where):
-        return pltpu.make_async_remote_copy(
-            src_ref=source, dst_ref=target, send_sem=halo_send.at[at],
-            recv_sem=halo_recv.at[at], device_id=where, device_id_type=MESH)
-
-    side = remote(colsend, colrecv.at[pl.ds(HALO, rows), :], 2, (emit, vx, other))
-
     def to_high():
         return (remote(rowsend.at[1], rowrecv.at[0], 0, (emit, vx + 1, vy)),
                 remote(colsend.at[pl.ds(rows - HALO, HALO), :], colrecv.at[pl.ds(0, HALO), :], 3,
@@ -140,7 +143,11 @@
         for copy in to_low():
             copy.start()
 
-    side.start()
+    for copy in lists:
+        copy.wait()
+    bits = jnp.int32(0)
+    for at in range(listed.shape[-1]):
+        bits = bits | lax.shift_left(jnp.int32(1), listed[0, 0, 0, at])
 
     @pl.when(has_high)
     def _():
@@ -264,6 +271,11 @@
                  + saved[1, col, place, :] * second)
         return total * (hit * (1.0 / n_emit))
 
+    def exchange(peer, slot):
+        return pltpu.make_async_remote_copy(
+            src_ref=outgoing.at[peer], dst_ref=incoming.at[slot], send_sem=block_send.at[peer],
+            recv_sem=block_recv.at[slot], device_id=(peer, vx, vy), device_id_type=MESH)
+
     def to_partner(at):
         return pltpu.make_async_remote_copy(
             src_ref=first_out.at[at], dst_ref=first_in.at[at], send_sem=first_send.at[at],
@@ -274,24 +286,36 @@
             src_ref=second_out.at[at], dst_ref=second_in.at[slot], send_sem=second_send.at[at],
             recv_sem=second_recv.at[slot], device_id=(2 * at + parity, vx, vy), device_id_type=MESH)
 
-    offsets = [half // 2 + at for at in range(half - half // 2)] + list(range(1, half // 2)) + [0]
-    order = [lax.rem(line + offset, half) for offset in offsets]
+    def fill(target, at, peer, slots):
+        parts = [masked(peer * per + slot) for slot in slots]
+        for which, part in enumerate(parts):
+            target[at, which] = part
+
+    offsets = [half // 2 + at for at in range(half - half // 2)] + list(range(1, half // 2))
+    order = [lax.rem(line + offset, half) for offset in offsets] + [line]
+    peers = [2 * at + side_of for at in order[:-1] for side_of in (parity, 1 - parity)] + [partner]
+    early, late = range(joint), range(joint, per)
 
     for at in order:
-        parts = [masked((2 * at + 1 - parity) * per + slot) for slot in range(per)]
-        for slot in range(per):
-            first_out[at, slot] = parts[slot]
+        fill(first_out, at, 2 * at + 1 - parity, early)
         to_partner(at).start()
+        if joint < per and at is not line:
+            fill(outgoing, 2 * at + parity, 2 * at + parity, late)
+            exchange(2 * at + parity, emit).start()
+    if joint < per:
+        for peer in peers[1::2] + [partner]:
+            fill(outgoing, peer, peer, late)
+            exchange(peer, emit).start()
     for at in order:
-        parts = [masked((2 * at + parity) * per + slot) for slot in range(per)]
-        for slot in range(per):
-            own_part[at, slot] = parts[slot]
+        fill(own_part, at, 2 * at + parity, early)
     for at in order[:-1]:
         to_partner(at).wait_recv()
         second_out[at] = own_part[at] + first_in[at]
         to_owner(at, line).start()
     to_partner(line).wait_recv()
     second_in[line] = own_part[line] + first_in[line]
+    if joint < per:
+        fill(incoming, emit, emit, late)
 
     def last_body(at, carry):
         row = TOP + at * CHUNK
@@ -323,12 +347,19 @@
 
     for at in range(half):
         to_partner(at).wait_send()
+    if joint < per:
+        for peer in peers[::-1]:
+            exchange(peer, peer).wait()
+        total = incoming[0]
+        for at in range(1, n_emit):
+            total = total + incoming[at]
+        grad[pl.ds(joint, per - joint)] = total
     for at in order[:-1]:
         to_owner(at, at).wait()
     total = second_in[0]
     for at in range(1, half):
         total = total + second_in[at]
-    grad[...] = total
+    grad[pl.ds(0, joint)] = total
     for copy in pres_copies:
         copy.wait()
 
@@ -356,18 +387,20 @@
     blocks = owner_map.shape[-1]
     per = blocks // n_emit
     half = n_emit // 2
+    joint = max(1, per // 2)
+    direct = max(1, per - joint)
     padded = rows + 2 * TOP
     anywhere = pl.BlockSpec(memory_space=pl.ANY)
-    scalars = pl.BlockSpec(memory_space=pltpu.SMEM)
-
-    def blocks_of(count):
-        return pltpu.VMEM((count, per, BR, BC), jnp.float32)
+    far = pl.BlockSpec(memory_space=pltpu.HBM)
+
+    def blocks_of(count, slots):
+        return pltpu.VMEM((count, slots, BR, BC), jnp.float32)
 
     found, waves = pl.pallas_call(
         functools.partial(kernel, n_emit, n_vx, rows),
         out_shape=(jax.ShapeDtypeStruct((per, BR, BC), jnp.float32),
                    jax.ShapeDtypeStruct((1, rows, 2 * BC), jnp.float32)),
-        in_specs=[anywhere] * 5 + [scalars] * 2,
+        in_specs=[far] * 7,
         out_specs=(pl.BlockSpec(memory_space=pltpu.VMEM), anywhere),
         scratch_shapes=[pltpu.VMEM((3, padded, BC), jnp.float32)] * ARRAYS + [
             pltpu.VMEM((4, 2, padded, BC), jnp.float32),
@@ -375,14 +408,19 @@
             pltpu.VMEM((2, 2, 40, BC), jnp.float32),
             pltpu.VMEM((rows, BC), jnp.float32),
             pltpu.VMEM((rows + 2 * HALO, BC), jnp.float32),
-        ] + [blocks_of(half)] * 5 + [
+        ] + [blocks_of(n_emit, direct)] * 2 + [blocks_of(half, joint)] * 5 + [
+            pltpu.SMEM(footprint.shape, jnp.int32),
+            pltpu.SMEM(owner_map.shape, jnp.int32),
             pltpu.SemaphoreType.DMA((2 * ARRAYS,)),
             pltpu.SemaphoreType.DMA((5,)),
             pltpu.SemaphoreType.DMA((5,)),
+            pltpu.SemaphoreType.DMA((n_emit,)),
+            pltpu.SemaphoreType.DMA((n_emit,)),
             pltpu.SemaphoreType.DMA((half,)),
             pltpu.SemaphoreType.DMA((half,)),
             pltpu.SemaphoreType.DMA((half,)),
             pltpu.SemaphoreType.DMA((half,)),
+            pltpu.SemaphoreType.DMA((2,)),
             pltpu.SemaphoreType.DMA((2,)),
         ],
         compiler_params=pltpu.CompilerParams(collective_id=0, has_side_effects=True),

time: 26 us -> 24.9 us (0.958)
  Pallas kernels: 25.2 us -> 24 us
    pallas_call x1, Pallas kernels: 23.5 us -> 22.4 us  [shards(): pl.pallas_call(functools.partial(kernel, n_emit, n_vx, rows), out_shape=(...]
where the time goes in v5:
time: 24.9 us; the launch traced here: 24.7 us
  Pallas kernels  24 us (96%)
  between operations  0.64 us (3%)
    pallas_call x1, Pallas kernels, shards(): pl.pallas_call(functools.partial(kernel, n_emit, n_vx, rows), out_shape=(...  22.4 us
    pallas_call x1, Pallas kernels, shards(): pl.pallas_call(hand_over, out_shape=(jax.ShapeDtypeStruct(found.shape, jn...  1.67 us

profile of v5, /device:TPU:0, one launch (start us, length us, event | category | flops | bytes accessed | tf_op | source)
XLA Modules:
  0.0 24.7 jit_solution(4239905415384944970)
XLA Ops:
  0.6 22.4 %waves.1 = (f32[4,16,128]{2,1,0:T(8,128)}, f32[1,256,256]{2,1,0:T(8,128)}) custom-call(f32[3,1,256,256]{3,2,1,0:T(8,128)} %fwd.1, f32[3,1,256,256]{3,2,1,0:T(8,128)} %adj.1, f32[256,256]{1,0:T(8,128)} %cour.1, f32[256,256]{1,0:T(8,128)} %dec.1, f32[256,256]{1,0:T(8,128)} %stren.1, s32[1,1,1,16]{3,2,1,0:T(1,128)} %listed_far.1, s32[1,1,32]{2,1,0:T(1,128)} %owner_far.1), custom_call_target="tpu_custom_call" | custom-call | tf_op jit(solution)/shard_map/waves/pallas_call | solution.py:399
  23.0 1.7 %hand_over.1 = (f32[4,16,128]{2,1,0:T(8,128)}, f32[1,256,256]{2,1,0:T(8,128)}) custom-call(f32[4,16,128]{2,1,0:T(8,128)} %get-tuple-element.4.found, f32[1,256,256]{2,1,0:T(8,128)} %get-tuple-element.5.waves), custom_call_target="tpu_custom_call" | custom-call | tf_op jit(solution)/shard_map/hand_over/pallas_call | solution.py:429

commit v6 on v4

--- a/solution.py
+++ b/solution.py
@@ -101,6 +101,18 @@
         return carry
 
     lax.fori_loop(0, rows // CHUNK, pack, 0)
+    near = (vx > 0).astype(jnp.int32) + (vx < n_vx - 1).astype(jnp.int32)
+    pl.semaphore_wait(barrier, n_emit + 2 * near)
+
+    def remote(source, target, at, where):
+        return pltpu.make_async_remote_copy(
+            src_ref=source, dst_ref=target, send_sem=halo_send.at[at],
+            recv_sem=halo_recv.at[at], device_id=where, device_id_type=MESH)
+
+    side = remote(colsend, colrecv.at[pl.ds(HALO, rows), :], 2, (emit, vx, other))
+
+    side.start()
+
     for copy in loads[ARRAYS:]:
         copy.wait()
     for which in range(ARRAYS):
@@ -109,16 +121,6 @@
             rowsend[0, col, place, :] = state[which][col, pl.ds(TOP, WIDE), :]
             rowsend[1, col, place, :] = state[which][col, pl.ds(end - WIDE, WIDE), :]
 
-    near = (vx > 0).astype(jnp.int32) + (vx < n_vx - 1).astype(jnp.int32)
-    pl.semaphore_wait(barrier, n_emit + 2 * near)
-
-    def remote(source, target, at, where):
-        return pltpu.make_async_remote_copy(
-            src_ref=source, dst_ref=target, send_sem=halo_send.at[at],
-            recv_sem=halo_recv.at[at], device_id=where, device_id_type=MESH)
-
-    side = remote(colsend, colrecv.at[pl.ds(HALO, rows), :], 2, (emit, vx, other))
-
     def to_high():
         return (remote(rowsend.at[1], rowrecv.at[0], 0, (emit, vx + 1, vy)),
                 remote(colsend.at[pl.ds(rows - HALO, HALO), :], colrecv.at[pl.ds(0, HALO), :], 3,
@@ -138,8 +140,6 @@
     def _():
         for copy in to_low():
             copy.start()
-
-    side.start()
 
     for copy in lists:
         copy.wait()

time: 24.7 us -> 24.7 us (level)
  no operation moved by 1% of the time
where the time goes in v6:
time: 24.7 us; the launch traced here: 24.5 us
  Pallas kernels  23.9 us (97%)
  between operations  0.64 us (3%)
    pallas_call x1, Pallas kernels, shards(): pl.pallas_call(functools.partial(kernel, n_emit, n_vx, rows), out_shape=(...  22.2 us
    pallas_call x1, Pallas kernels, shards(): pl.pallas_call(hand_over, out_shape=(jax.ShapeDtypeStruct(found.shape, jn...  1.67 us

profile of v6, /device:TPU:0, one launch (start us, length us, event | category | flops | bytes accessed | tf_op | source)
XLA Modules:
  0.0 24.5 jit_solution(4318389442047772009)
XLA Ops:
  0.6 22.2 %waves.1 = (f32[4,16,128]{2,1,0:T(8,128)}, f32[1,256,256]{2,1,0:T(8,128)}) custom-call(f32[3,1,256,256]{3,2,1,0:T(8,128)} %fwd.1, f32[3,1,256,256]{3,2,1,0:T(8,128)} %adj.1, f32[256,256]{1,0:T(8,128)} %cour.1, f32[256,256]{1,0:T(8,128)} %dec.1, f32[256,256]{1,0:T(8,128)} %stren.1, s32[1,1,1,16]{3,2,1,0:T(1,128)} %listed_far.1, s32[1,1,32]{2,1,0:T(1,128)} %owner_far.1), custom_call_target="tpu_custom_call" | custom-call | tf_op jit(solution)/shard_map/waves/pallas_call | solution.py:356
  22.9 1.7 %hand_over.1 = (f32[4,16,128]{2,1,0:T(8,128)}, f32[1,256,256]{2,1,0:T(8,128)}) custom-call(f32[4,16,128]{2,1,0:T(8,128)} %get-tuple-element.4.found, f32[1,256,256]{2,1,0:T(8,128)} %get-tuple-element.5.waves), custom_call_target="tpu_custom_call" | custom-call | tf_op jit(solution)/shard_map/hand_over/pallas_call | solution.py:382
